TPU v7x, 32 devices: a whole 2x2x4 slice. The times are simulated.
32 devices in a mesh: fsdp: 4 (over y, x), ctx: 2 (over core), tp: 4 (over z).
Axes of the slice: x: 2, y: 2, z: 4, core: 2. Of those that a mesh axis runs over, the one named last changes fastest.
Arguments:
- hidden: bfloat16 [4, 4096, 1024], P('fsdp', 'ctx'), may hold values from -6 to 6
- segments: int32 [4, 4096], P('fsdp', 'ctx'), may hold values from 0 to 8, as said below
- out_grad: bfloat16 [4, 4096, 1024], P('fsdp', 'ctx'), may hold values from -6 to 6
- norm_gain: bfloat16 [1024], P(('fsdp', 'ctx')), may hold values from 0.25 to 1.75
- w_zx: bfloat16 [1024, 2, 2048], P(('fsdp', 'ctx'), None, 'tp'), may hold values from -0.1875 to 0.1875
- w_dt: bfloat16 [1024, 32], P(('fsdp', 'ctx'), 'tp'), may hold values from -0.1875 to 0.1875
- w_bc: bfloat16 [1024, 2, 128], P(('fsdp', 'ctx')), may hold values from -0.1875 to 0.1875
- conv_x_w: float32 [4, 2048], P(None, 'tp'), may hold values from -3 to 3
- conv_x_b: float32 [2048], P('tp'), may hold values from -2 to 2
- conv_bc_w: float32 [4, 2, 128], replicated, may hold values from -3 to 3
- conv_bc_b: float32 [2, 128], replicated, may hold values from -2 to 2
- dt_bias: float32 [32], P('tp'), may hold values from -5 to -2
- a_log: float32 [32], P('tp'), may hold values from -3 to 1.4
- skip_d: float32 [32], P('tp'), may hold values from 0.5 to 1.5
- out_gain: float32 [2048], P('tp'), may hold values from 0.25 to 1.75
- w_out: bfloat16 [2048, 1024], P('tp', ('fsdp', 'ctx')), may hold values from -0.125 to 0.125
Outputs:
- block_out: bfloat16 [4, 4096, 1024], P('fsdp', 'ctx')
- hidden_grad: float32 [4, 4096, 1024], P('fsdp', 'ctx')
- norm_gain_grad: float32 [1024], P(('fsdp', 'ctx'))
- w_zx_grad: float32 [1024, 2, 2048], P(('fsdp', 'ctx'), None, 'tp')
- w_dt_grad: float32 [1024, 32], P(('fsdp', 'ctx'), 'tp')
- w_bc_grad: float32 [1024, 2, 128], P(('fsdp', 'ctx'))
- conv_x_w_grad: float32 [4, 2048], P(None, 'tp')
- conv_x_b_grad: float32 [2048], P('tp')
- conv_bc_w_grad: float32 [4, 2, 128], replicated
- conv_bc_b_grad: float32 [2, 128], replicated
- dt_bias_grad: float32 [32], P('tp')
- a_log_grad: float32 [32], P('tp')
- skip_d_grad: float32 [32], P('tp')
- out_gain_grad: float32 [2048], P('tp')
- w_out_grad: float32 [2048, 1024], P('tp', ('fsdp', 'ctx'))
Inputs may be any that keep to these rules, and one draw needn't show every extreme that they name: `segments`: in every sequence the segment numbers start at 0 and rise by 0 or 1 from one token to the next; every piece of 2048 tokens holds exactly 4 document starts, none at its first or last token, so that at every boundary between pieces the tokens on both sides lie in one document.
All inputs are finite; a program needn't handle non-finite values.
Results may differ from a plain program's by a relative error of at most 0.0099.
Values may be sent and summed in bfloat16 or wider, within the bound.
No kernel may reach another device: no remote copies, remote signals or barrier semaphores. Data moves between devices by JAX's collectives and lax.ppermute only.
A program may use at most 192 MiB of HBM per device.

v0:
```python
import jax
import jax.numpy as jnp
from jax import lax
from jax.sharding import PartitionSpec as P

BLOCK = 256


EPSILON = 1e-05
PRECISE = lax.Precision.HIGHEST


def passed_along(value, axis, steps):
    count = lax.axis_size(axis)
    leading, last = (max(0, -steps), min(count, count - steps))
    return lax.ppermute(value, axis, [(source, source + steps) for source in range(leading, last)])


def entering(value, axis, join, neutral):
    count, mine = (lax.axis_size(axis), lax.axis_index(axis))
    pieces = jax.tree.map(lambda part: lax.all_gather(part, axis), value)
    so_far = jax.tree.map(
        lambda part, zero: jnp.full_like(part, 0) + jnp.asarray(zero, part.dtype), value, neutral
    )

    def entering_turn(position, so_far):
        longer = join(so_far, jax.tree.map(lambda part: part[position], pieces))
        return jax.tree.map(lambda new, old: jnp.where(position < mine, new, old), longer, so_far)

    return lax.fori_loop(0, count - 1, entering_turn, so_far)


def carried_in_2(value, axis, combine, identity):
    devices, index = (lax.axis_size(axis), lax.axis_index(axis))
    everything = jax.tree.map(
        lambda part, kind: lax.all_gather(part.astype(kind), axis),
        value,
        jax.tree.map(lambda a: jnp.bfloat16 if a.dtype == jnp.float32 else a.dtype, value),
    )
    start = jax.tree.map(
        lambda part, zero: jnp.broadcast_to(jnp.asarray(zero, part.dtype), part.shape),
        value,
        identity,
    )

    def carried_turn(k, before):
        at = devices - 1 - k
        reached = at > index
        new = combine(
            before, jax.tree.map(lambda part, own: part[at].astype(own.dtype), everything, value)
        )
        return jax.tree.map(lambda a, b: jnp.where(reached, a, b), new, before)

    return lax.fori_loop(0, devices, carried_turn, start)


def causal_conv(values, weight, offset_bias, segment, edge_values, edge_segment):
    joined = jnp.concatenate([edge_values, values], 0)
    joined_segment = jnp.concatenate([edge_segment, segment], 0)
    length = values.shape[0]
    summed = jnp.zeros_like(values) + offset_bias
    for offset in range(weight.shape[0]):
        source = joined[offset : offset + length]
        same_doc = (joined_segment[offset : offset + length] == segment).astype(values.dtype)
        summed = summed + weight[offset] * source * same_doc[:, None]
    return summed


def block_step(carried_in, block_data):
    ssm_state, last_segment = carried_in
    values, input_b, input_c, step_size, decay_rate, segment = block_data
    cumulative = jnp.cumsum(decay_rate, axis=0)
    places = jnp.arange(segment.shape[0])
    linked = (segment[:, None] == segment[None, :]) & (places[:, None] >= places[None, :])
    gap_values = jnp.where(linked[:, :, None], cumulative[:, None, :] - cumulative[None, :, :], 0.0)
    decay_mask = jnp.where(linked[:, :, None], jnp.exp(gap_values), 0.0)
    scores = jnp.dot(input_c, input_b.T, precision=PRECISE, preferred_element_type=jnp.float32)
    weights = scores[:, :, None] * decay_mask * step_size[None, :, :]
    inside = jnp.einsum("tsh,shp->thp", weights, values, precision=PRECISE)
    entry_mask = (segment == last_segment).astype(jnp.float32)[:, None] * jnp.exp(cumulative)
    carried = (
        jnp.einsum("tn,hpn->thp", input_c, ssm_state, precision=PRECISE) * entry_mask[:, :, None]
    )
    linked_end = linked[-1].astype(jnp.float32)[:, None]
    tail_weight = linked_end * jnp.exp(cumulative[-1][None, :] - cumulative) * step_size
    new_state = entry_mask[-1][:, None, None] * ssm_state + jnp.einsum(
        "sh,shp,sn->hpn", tail_weight, values, input_b, precision=PRECISE
    )
    return ((new_state, segment[-1]), inside + carried)


def entry_weights(decay_rate, segment, edge_segment):
    cumulative = jnp.cumsum(decay_rate, axis=0)
    same_doc = (segment == edge_segment[-1]).astype(jnp.float32)
    return same_doc[:, None] * jnp.exp(cumulative)


def piece_front(
    small_params, inner_pre, state_pre, step_raw, edge_inner, edge_state, edge_segment, segment
):
    conv_x_w, conv_x_b, conv_bc_w, conv_bc_b, dt_bias, a_log = small_params
    inner_act = jax.nn.silu(
        causal_conv(inner_pre, conv_x_w, conv_x_b, segment, edge_inner, edge_segment)
    )
    state_act = jax.nn.silu(
        causal_conv(
            state_pre,
            conv_bc_w.reshape(conv_bc_w.shape[0], -1),
            conv_bc_b.reshape(-1),
            segment,
            edge_state,
            edge_segment,
        )
    )
    length = segment.shape[0]
    head_count = step_raw.shape[1]
    head_size = inner_pre.shape[1] // head_count
    state_size = state_pre.shape[1] // 2
    step_size = jax.nn.softplus(step_raw + dt_bias)
    decay_rate = -jnp.exp(a_log) * step_size
    values = inner_act.reshape(length, head_count, head_size)
    input_b = state_act[:, :state_size]
    input_c = state_act[:, state_size:]
    blocks = length // BLOCK
    stacked = (
        values.reshape(blocks, BLOCK, head_count, head_size),
        input_b.reshape(blocks, BLOCK, state_size),
        input_c.reshape(blocks, BLOCK, state_size),
        step_size.reshape(blocks, BLOCK, head_count),
        decay_rate.reshape(blocks, BLOCK, head_count),
        segment.reshape(blocks, BLOCK),
    )
    initial = (jnp.zeros((head_count, head_size, state_size), jnp.float32), edge_segment[-1])
    (local_state, _), outputs = lax.scan(jax.checkpoint(block_step), initial, stacked)
    return (
        values,
        input_c,
        decay_rate,
        outputs.reshape(length, head_count, head_size),
        local_state,
    )


def piece_rear(front_out, skip_d, gate_raw, state_in, edge_segment, segment):
    values, input_c, decay_rate, outputs, local_state = front_out
    entry_mask = entry_weights(decay_rate, segment, edge_segment)
    carried = (
        jnp.einsum("tn,hpn->thp", input_c, state_in, precision=PRECISE) * entry_mask[:, :, None]
    )
    scan_out = outputs + carried + skip_d[:, None] * values
    gated_inner = scan_out.reshape(gate_raw.shape) * jax.nn.silu(gate_raw)
    state_out = entry_mask[-1][:, None, None] * state_in + local_state
    return (gated_inner, state_out)


def chain_combine(earlier, later):
    return (earlier[0] * later[0], later[0][:, :, None, None] * earlier[1] + later[1])


def body(
    hidden,
    segments,
    out_grad,
    norm_gain,
    w_zx,
    w_dt,
    w_bc,
    conv_x_w,
    conv_x_b,
    conv_bc_w,
    conv_bc_b,
    dt_bias,
    a_log,
    skip_d,
    out_gain,
    w_out,
):
    gain_all, zx_all, step_all, bc_all, out_all = (
        lax.all_gather(norm_gain, ("fsdp", "ctx"), axis=0, tiled=True),
        lax.all_gather(w_zx, ("fsdp", "ctx"), axis=0, tiled=True),
        lax.all_gather(w_dt, ("fsdp", "ctx"), axis=0, tiled=True),
        lax.all_gather(w_bc, ("fsdp", "ctx"), axis=0, tiled=True),
        lax.all_gather(w_out, ("fsdp", "ctx"), axis=1, tiled=True),
    )
    seq_count, piece_len, model_width = hidden.shape
    row_count = seq_count * piece_len
    tokens = hidden.astype(jnp.float32).reshape(row_count, model_width)
    inv_rms = lax.rsqrt(jnp.mean(tokens * tokens, -1, keepdims=True) + EPSILON)
    unit_rows = tokens * inv_rms
    gain_float = gain_all.astype(jnp.float32)
    normed_low = (unit_rows * gain_float).astype(jnp.bfloat16)
    inner_local = zx_all.shape[2]
    head_local = step_all.shape[1]
    state_size = bc_all.shape[2]
    zx_flat = zx_all.reshape(model_width, 2 * inner_local)
    bc_flat = bc_all.reshape(model_width, 2 * state_size)
    zx_proj = jnp.dot(normed_low, zx_flat, preferred_element_type=jnp.float32)
    step_raw = jnp.dot(normed_low, step_all, preferred_element_type=jnp.float32).reshape(
        seq_count, piece_len, head_local
    )
    state_pre = jnp.dot(normed_low, bc_flat, preferred_element_type=jnp.float32).reshape(
        seq_count, piece_len, 2 * state_size
    )
    gate_raw = zx_proj[:, :inner_local].reshape(seq_count, piece_len, inner_local)
    inner_pre = zx_proj[:, inner_local:].reshape(seq_count, piece_len, inner_local)
    edge_count = conv_x_w.shape[0] - 1
    tail_start = piece_len - edge_count
    own_segment = segments[:, tail_start:].astype(jnp.float32)
    edge_inner, edge_state, edge_segment_float = passed_along(
        (inner_pre[:, tail_start:], state_pre[:, tail_start:], own_segment), "ctx", 1
    )
    edge_segment = edge_segment_float.astype(jnp.int32)
    small_params = (conv_x_w, conv_x_b, conv_bc_w, conv_bc_b, dt_bias, a_log)

    def front_all(params_in, inner_in, state_in_pre, step_in, edge_in, edge_state_in):
        return jax.vmap(piece_front, in_axes=(None, 0, 0, 0, 0, 0, 0, 0))(
            params_in,
            inner_in,
            state_in_pre,
            step_in,
            edge_in,
            edge_state_in,
            edge_segment,
            segments,
        )

    front_out, pull_front = jax.vjp(
        front_all, small_params, inner_pre, state_pre, step_raw, edge_inner, edge_state
    )
    input_c = front_out[1]
    local_state = front_out[4]
    entry_mask = jax.vmap(entry_weights)(front_out[2], segments, edge_segment)
    piece_decay = entry_mask[:, -1]
    scan_start = (jnp.ones_like(piece_decay), jnp.zeros_like(local_state))
    carried_state = entering((piece_decay, local_state), "ctx", chain_combine, scan_start)[1]

    def rear_all(front_in, skip_in, gate_in, state_given):
        return jax.vmap(piece_rear, in_axes=(0, None, 0, 0, 0, 0))(
            front_in, skip_in, gate_in, state_given, edge_segment, segments
        )

    (gated_inner, _), pull_rear = jax.vjp(rear_all, front_out, skip_d, gate_raw, carried_state)
    gated_flat = gated_inner.reshape(row_count, inner_local)
    inner_total = inner_local * lax.axis_size("tp")
    square_sum = lax.psum(jnp.sum(gated_flat * gated_flat, -1), "tp")
    inv_gate = lax.rsqrt(square_sum / inner_total + EPSILON)[:, None]
    gate_unit = gated_flat * inv_gate
    gate_low = (gate_unit * out_gain).astype(jnp.bfloat16)
    partial_out = jnp.dot(gate_low, out_all, preferred_element_type=jnp.float32)
    summed = lax.psum(partial_out, "tp")
    block_out = (tokens + summed).astype(jnp.bfloat16).reshape(seq_count, piece_len, model_width)
    contract_rows = (((0,), (0,)), ((), ()))
    contract_cols = (((1,), (1,)), ((), ()))
    cotangent = out_grad.reshape(row_count, model_width)
    out_w_grad = lax.dot_general(
        gate_low, cotangent, contract_rows, preferred_element_type=jnp.float32
    )
    d_gate = lax.dot_general(cotangent, out_all, contract_cols, preferred_element_type=jnp.float32)
    out_gain_grad = jnp.sum(d_gate * gate_unit, 0)
    scaled = d_gate * out_gain
    cross_sum = lax.psum(jnp.sum(scaled * gated_flat, -1), "tp")
    d_gated = inv_gate * scaled - gated_flat * inv_gate * inv_gate * inv_gate * (
        cross_sum[:, None] / inner_total
    )
    d_gated_seq = d_gated.reshape(seq_count, piece_len, inner_local)
    gate_silu = jax.nn.silu(gate_raw)
    d_scan = (d_gated_seq * gate_silu).reshape(seq_count, piece_len, head_local, -1)
    direct = jnp.einsum("stn,sth,sthp->shpn", input_c, entry_mask, d_scan, precision=PRECISE)
    later_grad = carried_in_2((piece_decay, direct), "ctx", chain_combine, scan_start)[1]
    d_front, d_skip, d_gate_raw, _ = pull_rear((d_gated_seq, later_grad))
    d_small, d_inner_pre, d_state_pre, d_step_raw, d_edge_inner, d_edge_state = pull_front(d_front)
    back_inner, back_state = passed_along((d_edge_inner, d_edge_state), "ctx", -1)
    d_inner_pre = d_inner_pre.at[:, tail_start:].add(back_inner)
    d_state_pre = d_state_pre.at[:, tail_start:].add(back_state)
    d_state_pre, d_conv_bc_w, d_conv_bc_b = lax.psum((d_state_pre, d_small[2], d_small[3]), "tp")
    d_zx_low = jnp.concatenate(
        [d_gate_raw.reshape(row_count, inner_local), d_inner_pre.reshape(row_count, inner_local)], 1
    ).astype(jnp.bfloat16)
    d_step_low = d_step_raw.reshape(row_count, head_local).astype(jnp.bfloat16)
    d_bc_low = d_state_pre.reshape(row_count, 2 * state_size).astype(jnp.bfloat16)
    zx_grad = lax.dot_general(
        normed_low, d_zx_low, contract_rows, preferred_element_type=jnp.float32
    ).reshape(model_width, 2, inner_local)
    step_grad = lax.dot_general(
        normed_low, d_step_low, contract_rows, preferred_element_type=jnp.float32
    )
    bc_grad = lax.dot_general(
        normed_low, d_bc_low, contract_rows, preferred_element_type=jnp.float32
    ).reshape(model_width, 2, state_size)
    head_part = lax.dot_general(
        d_zx_low, zx_flat, contract_cols, preferred_element_type=jnp.float32
    )
    head_part = head_part + lax.dot_general(
        d_step_low, step_all, contract_cols, preferred_element_type=jnp.float32
    )
    d_normed = lax.psum(head_part.astype(jnp.bfloat16), "tp").astype(jnp.float32)
    d_normed = d_normed + lax.dot_general(
        d_bc_low, bc_flat, contract_cols, preferred_element_type=jnp.float32
    )
    norm_gain_grad = jnp.sum(d_normed * unit_rows, 0)
    scaled_in = d_normed * gain_float
    cross_in = jnp.sum(scaled_in * tokens, -1, keepdims=True) / model_width
    hidden_grad = (
        cotangent.astype(jnp.float32)
        + inv_rms * scaled_in
        - unit_rows * inv_rms * inv_rms * cross_in
    )
    hidden_grad = hidden_grad.reshape(seq_count, piece_len, model_width)
    gain_grad, zx_owned, step_owned, bc_owned, out_owned = (
        lax.psum_scatter(norm_gain_grad, ("fsdp", "ctx"), scatter_dimension=0, tiled=True),
        lax.psum_scatter(zx_grad, ("fsdp", "ctx"), scatter_dimension=0, tiled=True),
        lax.psum_scatter(step_grad, ("fsdp", "ctx"), scatter_dimension=0, tiled=True),
        lax.psum_scatter(bc_grad, ("fsdp", "ctx"), scatter_dimension=0, tiled=True),
        lax.psum_scatter(out_w_grad, ("fsdp", "ctx"), scatter_dimension=1, tiled=True),
    )
    small_grads = lax.psum(
        (
            d_small[0],
            d_small[1],
            d_conv_bc_w,
            d_conv_bc_b,
            d_small[4],
            d_small[5],
            d_skip,
            out_gain_grad,
        ),
        ("fsdp", "ctx"),
    )
    return (
        block_out,
        hidden_grad,
        gain_grad,
        zx_owned,
        step_owned,
        bc_owned,
        small_grads[0],
        small_grads[1],
        small_grads[2],
        small_grads[3],
        small_grads[4],
        small_grads[5],
        small_grads[6],
        small_grads[7],
        out_owned,
    )


def solution(mesh):
    placed = (
        P("fsdp", "ctx", None),
        P("fsdp", "ctx"),
        P("fsdp", "ctx", None),
        P(("fsdp", "ctx")),
        P(("fsdp", "ctx"), None, "tp"),
        P(("fsdp", "ctx"), "tp"),
        P(("fsdp", "ctx"), None, None),
        P(None, "tp"),
        P("tp"),
        P(),
        P(),
        P("tp"),
        P("tp"),
        P("tp"),
        P("tp"),
        P("tp", ("fsdp", "ctx")),
    )
    return jax.shard_map(
        body,
        mesh=mesh,
        in_specs=placed,
        out_specs=(
            P("fsdp", "ctx", None),
            P("fsdp", "ctx", None),
            P(("fsdp", "ctx")),
            P(("fsdp", "ctx"), None, "tp"),
            P(("fsdp", "ctx"), "tp"),
            P(("fsdp", "ctx"), None, None),
            P(None, "tp"),
            P("tp"),
            P(),
            P(),
            P("tp"),
            P("tp"),
            P("tp"),
            P("tp"),
            P("tp", ("fsdp", "ctx")),
        ),
        check_vma=False,
    )
```

profile of v0, /device:TPU:0, one launch (start us, length us, event | category | flops | bytes accessed | tf_op | source)
XLA Modules:
  0.0 1467.2 jit_solution(10770733252255792515)
XLA Ops:
  11.3 9.7 all-gather.2
  21.0 9.9 all_gather.37
  38.1 8.4 all_gather.35
  68.4 5.3 copy.275
  96.3 5.4 copy.246
  109.1 230.4 %while.71 = (s32[]{:T(128)}, f32[1,8,64,128]{3,2,1,0:T(8,128)S(1)}, s32[1]{0:T(128)}, f32[8,1,256,8,64]{2,0,4,3,1:T(8,128)}, f32[8,1,8,64,128]{4,3,2,1,0:T(8,128...) while((s32[]{:T(128)}, f32[1,8,64,128]{3,2,1,0:T(8,128)S(1)}, ...), condition=%wide.region_4.5_spmd.clone.clone, body=%wide.region_1.4_spmd.clone.clone.sunk | while | flops 909847808 | bytes 7446213 | solution.py:134
  118.5 12.7 dynamic_update_slice.94
  147.3 12.7 dynamic_update_slice.94
  176.1 12.7 dynamic_update_slice.94
  204.9 12.7 dynamic_update_slice.94
  233.7 12.7 dynamic_update_slice.94
  262.5 12.7 dynamic_update_slice.94
  291.3 12.7 dynamic_update_slice.94
  320.1 12.7 dynamic_update_slice.94
  354.1 5.3 copy.258
  359.5 6.6 multiply_reduce_fusion.9
  366.0 12.1 psum.105
  378.2 9.3 multiply_reduce_fusion.2
  387.5 8.9 psum.107
  396.5 8.4 fusion.148
  406.7 7.0 fusion.158
  413.7 7.0 reshape.1722
  420.7 5.4 copy.260
  426.1 6.8 copy.269
  432.9 5.6 fusion.189
  445.6 211.1 %while.69 = (s32[]{:T(128)}, f32[1,8,64,128]{3,2,1,0:T(8,128)S(1)}, f32[8,1,256,8,64]{2,4,3,1,0:T(8,128)}, f32[8,1,256,128]{3,2,0,1:T(8,128)}, f32[8,1,256,128]{...) while((s32[]{:T(128)}, f32[1,8,64,128]{3,2,1,0:T(8,128)S(1)}, ...), condition=%wide.region_26.27_spmd, body=%wide.region_14.26_spmd.sunk | while | flops 2126622464 | bytes 15416521 | solution.py:134
  656.7 7.0 copy.293
  663.6 7.5 reshape.1723
  671.2 12.9 multiply_reduce_fusion.5
  691.5 5.7 pad_add_fusion
  705.0 9.9 reduce-window.80
  715.1 6.5 mul.1155
  721.6 5.4 copy.276
  727.0 8.7 fusion.178
  754.8 80.8 %all-reduce.31 = (bf16[1,2048,256]{2,1,0:T(8,128)(2,1)S(1)}, f32[4,2,128]{2,1,0:T(2,128)S(1)}, f32[2,128]{1,0:T(2,128)S(1)}) all-reduce(f32[1,2048,256]{2,1,0:T(8,128)} %scatter-add.9, f32[4,2,128]{2,1,0:T(2,128)S(1)} %reshape.1666, f32[2,128]{1,0:T(2,128)S(1)} %bitcast.914), channel_id=1, replica_groups=mesh['fsdp'=4,'ctx'=2,'tp'=4] {'tp'}, use_global_device_ids=true, to_apply=%region_32.33 | all-reduce | flops 525568 | bytes 3155968 | tf_op jit(solution)/shard_map/psum | solution.py:275
  843.0 6.8 fusion.176
  857.5 6.7 copy.295
  864.2 10.5 fusion.156
  875.9 7.8 fusion.234
  888.2 7.3 fusion.159
  898.7 134.9 %all-reduce.30.cloned.1.call-done = bf16[2048,1024]{1,0:T(8,128)(2,1)} async-done(((bf16[2048,1024]{1,0:T(8,128)(2,1)}), bf16[2048,1024]{1,0:T(8,128)(2,1)}) %all-reduce.30.cloned.1.call-update) | async-done | bytes 4194320 | tf_op jit(solution)/shard_map/psum | solution.py:296
  1033.6 7.5 fusion.138
  1041.1 24.8 %all-reduce.22 = (f32[1024]{0:T(1024)S(1)}, f32[4,512]{1,0:T(4,128)}, f32[512]{0:T(512)}, f32[4,2,128]{2,1,0:T(2,128)}, f32[2,128]{1,0:T(2,128)}, /*index=5*/f32...) all-reduce(f32[1024]{0:T(1024)S(1)} %get-tuple-element.1057, ...), channel_id=4, replica_groups=mesh['fsdp'=4,'ctx'=2,'tp'=4] {'fsdp','ctx'}, use_global_device_ids=true, to_apply=%region_35.36.clone | all-reduce | flops 5400 | bytes 43200
  1066.5 21.1 %reduce-scatter.5.cloned.1.call-done = f32[128,2,512]{2,0,1:T(8,128)} async-done(((f32[1024,2,512]{2,0,1:T(8,128)}), f32[128,2,512]{2,0,1:T(8,128)}) %reduce-scatter.5.cloned.1.call-update) | async-done | bytes 524304 | tf_op jit(solution)/shard_map/reduce_scatter | solution.py:311
  1089.8 290.9 %all-reduce.28.cloned.1.call-done = f32[2048,1024]{1,0:T(8,128)} async-done(((f32[2048,1024]{1,0:T(8,128)}), f32[2048,1024]{1,0:T(8,128)}) %all-reduce.28.cloned.1.call-update) | async-done | bytes 8388624 | tf_op jit(solution)/shard_map/psum | solution.py:250
  1380.8 14.9 %fusion.137 = (f32[1,2048,1024]{2,1,0:T(8,128)}, bf16[1,2048,1024]{2,1,0:T(8,128)(2,1)}) fusion(bf16[1,2048,1024]{2,1,0:T(8,128)(2,1)} %param.26, f32[2048,1024]{1,0:T(8,128)} %get-tuple-element.1206, bf16[1,2048,1024]{2,1,0:T(8,128)(2,1)} %param.28, f32[2048]{0:T(1024)S(1)} %broadcast_multiply_fusion.4, f32[1024]{0:T(1024)S(1)} %bitcast.907, ...), kind=kLoop, calls=%fused_computation.191 | loop fusion | flops 25165824 | bytes 37769216 | tf_op jit(solution)/shard_map/reshape | solution.py:308
  1395.7 19.0 %reduce-scatter.7.cloned.1.call-done = f32[128,8]{0,1:T(8,128)} async-done(((f32[1024,8]{0,1:T(8,128)}), f32[128,8]{0,1:T(8,128)}) %reduce-scatter.7.cloned.1.call-update) | async-done | bytes 4112 | tf_op jit(solution)/shard_map/reduce_scatter | solution.py:312
  1414.7 45.5 %reduce-scatter.11.cloned.1.call-done = f32[512,128]{1,0:T(8,128)} async-done(((f32[512,1024]{1,0:T(8,128)}), f32[512,128]{1,0:T(8,128)}) %reduce-scatter.11.cloned.1.call-update) | async-done | bytes 262160 | tf_op jit(solution)/shard_map/reduce_scatter | solution.py:314
  (842 shorter events, 479.3 us)
Async XLA Ops:
  7.2 70.2 %all-gather.6.cloned.1.call-start = ((), (), s32[]{:S(2)}) async-start(), calls=%async_computation.4 | async-start | bytes 2359296 | tf_op jit(solution)/shard_map/all_gather | solution.py:180
  7.9 370.3 %all-gather.8.cloned.1.call-start = ((), (), s32[]{:S(2)}) async-start(), calls=%async_computation.5 | async-start | bytes 1179648 | tf_op jit(solution)/shard_map/all_gather | solution.py:183
  8.0 26.3 %copy-start.18 = (bf16[1,2048,1024]{2,1,0:T(8,128)(2,1)S(1)}, bf16[1,2048,1024]{2,1,0:T(8,128)(2,1)}, u32[]{:S(2)}) copy-start(bf16[1,2048,1024]{2,1,0:T(8,128)(2,1)} %param.26) | copy-start | bytes 12582916
  8.9 46.7 %collective-permute-start = (f32[1,3]{1,0:T(1,128)S(1)}, f32[1,3]{1,0:T(1,128)S(1)}, u32[]{:S(2)}, u32[]{:S(2)}) collective-permute-start(f32[1,3]{1,0:T(1,128)S(1)} %slice_convert_fusion), channel_id=1, source_target_pairs={{0,4},{1,5},{2,6},{3,7},{8,12},{9,13},{10,14},{11,15},{16,20},{17,... | collective-permute-start | bytes 44 | tf_op jit(solution)/shard_map/ppermute | solution.py:16
  21.0 58.7 %copy-start.60 = (f32[8,1,128]{2,1,0:T(1,128)}, f32[8,1,128]{2,1,0:T(1,128)S(1)}, u32[]{:S(2)}) copy-start(f32[8,1,128]{2,1,0:T(1,128)S(1)} %convert_element_type.191) | copy-start | bytes 12292
  34.2 45.5 %copy-start.46 = (f32[2048]{0:T(1024)}, f32[2048]{0:T(1024)S(1)}, u32[]{:S(2)}) copy-start(f32[2048]{0:T(1024)S(1)} %add_rsqrt_fusion.1) | copy-start | bytes 24580
  34.3 12.2 copy-start.82
  34.3 12.2 copy-start.81
  35.7 38.1 %copy-start.10 = (f32[2048,256]{1,0:T(8,128)}, f32[2048,256]{1,0:T(8,128)S(1)}, u32[]{:S(2)}) copy-start(f32[2048,256]{1,0:T(8,128)S(1)} %fusion.165) | copy-start | bytes 6291460
  35.7 38.1 %collective-permute-start.2 = (f32[1,3,256]{2,1,0:T(4,128)S(1)}, f32[1,3,256]{2,1,0:T(4,128)S(1)}, u32[]{:S(2)}, u32[]{:S(2)}) collective-permute-start(f32[1,3,256]{2,1,0:T(4,128)S(1)} %slice.314), channel_id=1, source_target_pairs={{0,4},{1,5},{2,6},{3,7},{8,12},{9,13},{10,14},{11,15},{16,20},{17,... | collective-permute-start | bytes 9224 | tf_op jit(solution)/shard_map/ppermute | solution.py:16
  38.0 859.1 %reduce-scatter.9.cloned.1.call-start = ((), (), s32[]{:S(2)}) async-start(), calls=%async_computation.10 | async-start | bytes 1179648 | tf_op jit(solution)/shard_map/reduce_scatter | solution.py:313
  54.5 36.4 %copy-start.50 = (f32[1,512]{1,0:T(1,128)}, f32[1,512]{1,0:T(1,128)S(1)}, u32[]{:S(2)}) copy-start(f32[1,512]{1,0:T(1,128)S(1)} %get-tuple-element.1196) | copy-start | bytes 6148
  54.5 36.4 %copy-start.52 = (f32[1,512]{1,0:T(1,128)}, f32[1,512]{1,0:T(1,128)S(1)}, u32[]{:S(2)}) copy-start(f32[1,512]{1,0:T(1,128)S(1)} %get-tuple-element.1197) | copy-start | bytes 6148
  54.5 36.4 %copy-start.54 = (f32[1,512]{1,0:T(1,128)}, f32[1,512]{1,0:T(1,128)S(1)}, u32[]{:S(2)}) copy-start(f32[1,512]{1,0:T(1,128)S(1)} %get-tuple-element.1198) | copy-start | bytes 6148
  54.5 36.4 %copy-start.56 = (f32[1,512]{1,0:T(1,128)}, f32[1,512]{1,0:T(1,128)S(1)}, u32[]{:S(2)}) copy-start(f32[1,512]{1,0:T(1,128)S(1)} %get-tuple-element.1199) | copy-start | bytes 6148
  54.5 19.3 %copy-start.62 = (f32[256]{0:T(256)}, f32[256]{0:T(256)S(1)}, u32[]{:S(2)}) copy-start(f32[256]{0:T(256)S(1)} %get-tuple-element.1200) | copy-start | bytes 3076
  54.5 19.3 %copy-start.64 = (f32[256]{0:T(256)}, f32[256]{0:T(256)S(1)}, u32[]{:S(2)}) copy-start(f32[256]{0:T(256)S(1)} %get-tuple-element.1201) | copy-start | bytes 3076
  54.6 19.3 %copy-start.66 = (f32[256]{0:T(256)}, f32[256]{0:T(256)S(1)}, u32[]{:S(2)}) copy-start(f32[256]{0:T(256)S(1)} %get-tuple-element.1202) | copy-start | bytes 3076
  54.6 19.3 %copy-start.68 = (f32[256]{0:T(256)}, f32[256]{0:T(256)S(1)}, u32[]{:S(2)}) copy-start(f32[256]{0:T(256)S(1)} %get-tuple-element.1203) | copy-start | bytes 3076
  54.8 19.0 %copy-start.36 = (f32[8,16]{0,1:T(8,128)}, f32[8,16]{0,1:T(8,128)S(1)}, u32[]{:S(2)}) copy-start(f32[8,16]{0,1:T(8,128)S(1)} %copy.255) | copy-start | bytes 1540
  57.8 16.0 %copy-start.38 = (f32[1,2048]{1,0:T(1,128)}, f32[1,2048]{1,0:T(1,128)S(1)}, u32[]{:S(2)}) copy-start(f32[1,2048]{1,0:T(1,128)S(1)} %get-tuple-element.1195) | copy-start | bytes 24580
  62.1 284.8 %copy-start.48 = (f32[8]{0:T(128)}, f32[8]{0:T(128)S(1)}, u32[]{:S(2)}) copy-start(f32[8]{0:T(128)S(1)} %fusion.228) | copy-start | bytes 100
  86.4 9.9 copy-start.7
  86.5 4.4 collective-permute-start.1
  359.5 18.7 %copy-start.45 = (f32[512]{0:T(512)S(1)}, f32[512]{0:T(512)}, u32[]{:S(2)}) copy-start(f32[512]{0:T(512)} %param.40) | copy-start | bytes 6148
  396.5 9.1 copy-start.8
  396.5 10.2 copy-start.21
  671.1 12.9 copy-start.51
  671.1 12.9 copy-start.53
  671.1 12.9 copy-start.55
  671.2 12.9 copy-start.57
  727.0 8.7 copy-start.11
  727.0 8.7 copy-start.24
  727.0 8.8 copy-start.30
  727.0 8.8 copy-start.59
  744.3 97.0 %collective-permute-start.3 = (f32[1,3,512]{2,1,0:T(4,128)S(1)}, f32[1,3,512]{2,1,0:T(4,128)S(1)}, u32[]{:S(2)}, u32[]{:S(2)}) collective-permute-start(f32[1,3,512]{2,1,0:T(4,128)S(1)} %pad_add_fusion.2), channel_id=1, source_target_pairs={{4,0},{5,1},{6,2},{7,3},{12,8},{13,9},{14,10},{15,11},{20,16},{21,... | collective-permute-start | bytes 18440 | tf_op jit(solution)/shard_map/ppermute | solution.py:16
  748.0 4.8 collective-permute-start.4
  753.5 82.8 %copy-start.47 = (f32[2048]{0:T(1024)S(1)}, f32[2048]{0:T(1024)}, u32[]{:S(2)}) copy-start(f32[2048]{0:T(1024)} %copy-done.46) | copy-start | bytes 24580
  753.5 82.8 %copy-start.61 = (f32[8,1,128]{2,1,0:T(1,128)S(1)}, f32[8,1,128]{2,1,0:T(1,128)}, u32[]{:S(2)}) copy-start(f32[8,1,128]{2,1,0:T(1,128)} %copy-done.60) | copy-start | bytes 12292
  841.3 192.3 %all-reduce.30.cloned.1.call-start = ((), (), s32[]{:S(2)}) async-start(), calls=%async_computation.7 | async-start | bytes 8388608 | tf_op jit(solution)/shard_map/psum | solution.py:296
  853.2 234.4 %reduce-scatter.5.cloned.1.call-start = ((), (), s32[]{:S(2)}) async-start(), calls=%async_computation.8 | async-start | bytes 4718592 | tf_op jit(solution)/shard_map/reduce_scatter | solution.py:311
  874.7 506.1 %all-reduce.28.cloned.1.call-start = ((), (), s32[]{:S(2)}) async-start(), calls=%async_computation.6 | async-start | bytes 16777216 | tf_op jit(solution)/shard_map/psum | solution.py:250
  883.7 531.0 %reduce-scatter.7.cloned.1.call-start = ((), (), s32[]{:S(2)}) async-start(), calls=%async_computation.9 | async-start | bytes 36864 | tf_op jit(solution)/shard_map/reduce_scatter | solution.py:312
  888.1 8.7 copy-start.70
  888.1 8.9 copy-start.83
  888.1 145.5 %copy-start.34 = (bf16[1024,2,128]{2,1,0:T(2,128)(2,1)S(1)}, bf16[1024,2,128]{2,1,0:T(2,128)(2,1)}, u32[]{:S(2)}) copy-start(bf16[1024,2,128]{2,1,0:T(2,128)(2,1)} %copy-done.33) | copy-start | bytes 1572868
  888.1 572.0 %reduce-scatter.11.cloned.1.call-start = ((), (), s32[]{:S(2)}) async-start(), calls=%async_computation.11 | async-start | bytes 2359296 | tf_op jit(solution)/shard_map/reduce_scatter | solution.py:314
  898.7 142.4 %copy-start.77 = (f32[512]{0:T(512)S(1)}, f32[512]{0:T(512)}, u32[]{:S(2)}) copy-start(f32[512]{0:T(512)} %get-tuple-element.1062) | copy-start | bytes 6148
  (57 other events, 250.4 us)
Sparse Core Ops, SparseCore 0:
  9.9 30.7 all-gather.5
  42.6 23.6 all-gather.7
  841.4 34.3 reduce-scatter.8
  878.6 154.9 all-reduce.29
  1037.2 50.3 reduce-scatter.4
  1089.9 290.8 all-reduce.27
  1384.3 30.2 reduce-scatter.6
  1418.9 41.2 reduce-scatter.10
where the time goes:
time: 1480 us; the launch traced here: 1470 us
  waiting for transfers between devices  512 us (35%)
  local copies, waits for them, and re-layouts  318 us (21%)
  matrix products  259 us (18%)
  other arithmetic  181 us (12%)
  blocking collectives  163 us (11%)
  between operations  16.4 us (1%)
    psum x1, waiting for transfers between devices, body(): summed = lax.psum(partial_out, 'tp')  291 us
    psum x1, waiting for transfers between devices, body(): lax.psum(head_part.astype(jnp.bfloat16), 'tp').astype(jnp.float32)  135 us
    dynamic_update_slice x40, local copies, waits for them, and re-layouts, piece_front(): lax.scan(jax.checkpoint(block_step), initial, stacked)  123 us
    dot_general x24, matrix products, block_step(): inside = jnp.einsum('tsh,shp->thp', weights, values, precision=PRECISE)  90.3 us
    psum x1, blocking collectives, body(): lax.psum((d_state_pre, d_small[2], d_small[3]), 'tp')  80.8 us
    another operation x71, other arithmetic  58.1 us
    reduce_scatter x1, waiting for transfers between devices, body(): lax.psum_scatter(out_w_grad, ('fsdp', 'ctx'), scatter_dimension=1, tiled=...  45.5 us
    squeeze x48, local copies, waits for them, and re-layouts, piece_front(): lax.scan(jax.checkpoint(block_step), initial, stacked)  37.2 us
  transfers between devices with their start and end apart: 13, of which 5 were waited for; matrix products, arithmetic and copies ran while one was open for 27% of the time, Pallas kernels for 0%

commit v1 on v0

v1 whole, which is shorter than its diff:
```python
import functools

import jax
import jax.numpy as jnp
from jax import lax
from jax.experimental import pallas as pl
from jax.experimental.pallas import tpu as pltpu
from jax.sharding import PartitionSpec as P

CHUNK = 128
STEP = 256
SUB = STEP // CHUNK
LANES = 128
EDGE = 16
GROUPS = 4
EPSILON = 1e-05
EXACT = lax.Precision.HIGHEST
F32 = jnp.float32
BF16 = jnp.bfloat16
NEGATIVE = -1e30
M1, M2, M3, ENTRY, TAIL, SEG, RAW = 16, 17, 18, 19, 20, 21, 24
VMEM_LIMIT = 56 * 1024 * 1024


def nn(a, b):
    return lax.dot_general(a, b, (((1,), (0,)), ((), ())), preferred_element_type=F32)


def nt(a, b):
    return lax.dot_general(a, b, (((1,), (1,)), ((), ())), preferred_element_type=F32)


def tn(a, b):
    return nn(a.T, b)


def exact(a, b):
    return lax.dot_general(
        a, b, (((1,), (0,)), ((), ())), precision=EXACT, preferred_element_type=F32
    )


def iota(shape, dim):
    return lax.broadcasted_iota(jnp.int32, shape, dim)


def spread(per_head, pairs):
    rows = per_head.shape[0]
    low = iota((rows, LANES), 1) < LANES // 2
    parts = []
    for j in range(pairs):
        left = jnp.broadcast_to(per_head[:, 2 * j : 2 * j + 1], (rows, LANES))
        right = jnp.broadcast_to(per_head[:, 2 * j + 1 : 2 * j + 2], (rows, LANES))
        parts.append(jnp.where(low, left, right))
    return jnp.concatenate(parts, 1)


def halves(block):
    low = iota(block.shape, 1) < LANES // 2
    zero = jnp.zeros_like(block)
    return jnp.where(low, block, zero), jnp.where(low, zero, block)


def silu(v):
    return v * jax.nn.sigmoid(v)


def rms_unit(x):
    return x * lax.rsqrt(jnp.mean(x * x, -1, keepdims=True) + EPSILON)


def front_kernel(
    hid, edge, tok, w, gain, cw, dtp,
    normed, gate, pre_out, u_out, rec, st, pdx, fin, pdfin,
    buf, state, decay,
):
    inner = gate.shape[1]
    wide = pre_out.shape[1]
    pairs = inner // LANES
    at = pl.program_id(0)

    @pl.when(at == 0)
    def _():
        edge_low = (rms_unit(edge[...].astype(F32)) * gain[...]).astype(BF16)
        edge_pre = nn(edge_low, w[:, inner : inner + wide])
        buf[0:8, :] = edge_pre[EDGE - 8 :, :]
        state[...] = jnp.zeros_like(state)
        decay[...] = jnp.ones_like(decay)

    @pl.when(at > 0)
    def _():
        buf[0:8, :] = buf[STEP : STEP + 8, :]

    low = (rms_unit(hid[...].astype(F32)) * gain[...]).astype(BF16)
    normed[...] = low
    gate[...] = nn(low, w[:, :inner])
    pre = nn(low, w[:, inner : inner + wide])
    pre_out[...] = pre
    buf[8 : 8 + STEP, :] = pre
    raw_all = nn(low, w[:, inner + wide :]) + dtp[0:1, :]
    marks = tok[...]
    u = cw[3:4, :] * pre + cw[4:5, :]
    u = u + cw[2:3, :] * (buf[7 : 7 + STEP, :] * marks[:, M1 : M1 + 1])
    u = u + cw[1:2, :] * (buf[6 : 6 + STEP, :] * marks[:, M2 : M2 + 1])
    u = u + cw[0:1, :] * (buf[5 : 5 + STEP, :] * marks[:, M3 : M3 + 1])
    u_out[...] = u
    act = silu(u)
    step_all = jax.nn.softplus(raw_all)
    lane = iota((CHUNK, LANES), 1)
    lower = (iota((CHUNK, CHUNK), 0) >= iota((CHUNK, CHUNK), 1)).astype(F32)
    for i in range(SUB):
        rows = slice(i * CHUNK, (i + 1) * CHUNK)
        step = step_all[rows]
        cum = exact(lower, step * dtp[1:2, :])
        mark = marks[rows]
        rec[rows, :] = jnp.where(
            lane < 8, cum, jnp.where(lane < 16, step, jnp.where(lane < 24, mark, raw_all[rows]))
        )
        last = cum[CHUNK - 1 :, :]
        tail = mark[:, TAIL : TAIL + 1] * jnp.exp(last - cum) * step
        fed = (act[rows, :inner] * spread(tail, pairs)).astype(BF16)
        st[i] = state[...]
        pdx[8 * i : 8 * i + 8, :] = decay[...]
        passed = spread(mark[CHUNK - 1 :, ENTRY : ENTRY + 1] * jnp.exp(last), pairs)
        input_b = act[rows, inner : inner + LANES].T.astype(BF16)
        state[...] = passed * state[...] + nn(input_b, fed)
        decay[...] = decay[...] * passed
    fin[...] = state[...]
    pdfin[...] = decay[...]


def front(hidden, edge, tok, w, gain, cw, dtp, inner, wide):
    rows, width = hidden.shape
    steps = rows // STEP
    state_size = LANES

    def whole(a):
        return pl.BlockSpec(a.shape, lambda i: (0,) * a.ndim)

    def tall(cols):
        return pl.BlockSpec((STEP, cols), lambda i: (i, 0))

    chunks = rows // CHUNK
    return pl.pallas_call(
        front_kernel,
        grid=(steps,),
        in_specs=[tall(width), whole(edge), tall(LANES), whole(w), whole(gain), whole(cw), whole(dtp)],
        out_specs=[
            tall(width),
            tall(inner),
            tall(wide),
            tall(wide),
            tall(LANES),
            pl.BlockSpec((SUB, state_size, inner), lambda i: (i, 0, 0)),
            pl.BlockSpec((8 * SUB, inner), lambda i: (i, 0)),
            pl.BlockSpec((state_size, inner), lambda i: (0, 0)),
            pl.BlockSpec((8, inner), lambda i: (0, 0)),
        ],
        out_shape=[
            jax.ShapeDtypeStruct((rows, width), BF16),
            jax.ShapeDtypeStruct((rows, inner), F32),
            jax.ShapeDtypeStruct((rows, wide), F32),
            jax.ShapeDtypeStruct((rows, wide), F32),
            jax.ShapeDtypeStruct((rows, LANES), F32),
            jax.ShapeDtypeStruct((chunks, state_size, inner), F32),
            jax.ShapeDtypeStruct((8 * chunks, inner), F32),
            jax.ShapeDtypeStruct((state_size, inner), F32),
            jax.ShapeDtypeStruct((8, inner), F32),
        ],
        scratch_shapes=[
            pltpu.VMEM((STEP + 8, wide), F32),
            pltpu.VMEM((state_size, inner), F32),
            pltpu.VMEM((8, inner), F32),
        ],
        compiler_params=pltpu.CompilerParams(
            dimension_semantics=("arbitrary",), vmem_limit_bytes=VMEM_LIMIT
        ),
        name="front",
    )(hidden, edge, tok, w, gain, cw, dtp)


def middle_kernel(
    u, rec, gate, st, pdx, sin, og, wo, prm,
    scan, dgate, sums, part,
):
    inner = gate.shape[1]
    pairs = inner // LANES
    d_gate = nn(og[...], wo[...])
    dgate[...] = d_gate
    act = silu(u[...])
    below = iota((CHUNK, CHUNK), 0) >= iota((CHUNK, CHUNK), 1)
    for i in range(SUB):
        rows = slice(i * CHUNK, (i + 1) * CHUNK)
        record = rec[rows, :]
        turned = record.T
        state = (st[i] + pdx[8 * i : 8 * i + 1, :] * sin[...]).astype(BF16)
        x = act[rows, :inner]
        input_b = act[rows, inner : inner + LANES].astype(BF16)
        input_c = act[rows, inner + LANES :].astype(BF16)
        scores = nt(input_c, input_b)
        barred = jnp.where(
            below & (record[:, SEG : SEG + 1] == turned[SEG : SEG + 1, :]), 0.0, NEGATIVE
        )
        entry = record[:, ENTRY : ENTRY + 1] * jnp.exp(record)
        outs = []
        for j in range(pairs):
            block = x[:, j * LANES : (j + 1) * LANES].astype(BF16)
            total = None
            for k, side in enumerate(halves(block)):
                h = 2 * j + k
                link = jnp.exp(record[:, h : h + 1] - turned[h : h + 1, :] + barred)
                weight = (scores * link * turned[8 + h : 9 + h, :]).astype(BF16)
                term = nn(weight, side)
                total = term if total is None else total + term
            outs.append(total)
        y = jnp.concatenate(outs, 1)
        y = y + nn(input_c, state) * spread(entry, pairs) + prm[0:1, :] * x
        scan[rows, :] = y
    gated = scan[...] * silu(gate[...])
    scaled = gated * prm[1:2, :]
    squares = jnp.sum(gated * gated, -1, keepdims=True)
    crosses = jnp.sum(scaled * d_gate, -1, keepdims=True)
    lane = iota((STEP, LANES), 1)
    both = jnp.where(lane == 0, squares, jnp.where(lane == 1, crosses, 0.0))
    sums[...] = both.T[0:8, :]
    part[...] = nt(scaled.astype(BF16), wo[...]).astype(BF16)


def middle(u, rec, gate, st, pdx, sin, og, wo, prm):
    rows, inner = gate.shape
    width = og.shape[1]

    def whole(a):
        return pl.BlockSpec(a.shape, lambda i: (0,) * a.ndim)

    def tall(cols):
        return pl.BlockSpec((STEP, cols), lambda i: (i, 0))

    return pl.pallas_call(
        middle_kernel,
        grid=(rows // STEP,),
        in_specs=[
            tall(u.shape[1]),
            tall(LANES),
            tall(inner),
            pl.BlockSpec((SUB,) + st.shape[1:], lambda i: (i, 0, 0)),
            pl.BlockSpec((8 * SUB, inner), lambda i: (i, 0)),
            whole(sin),
            tall(width),
            whole(wo),
            whole(prm),
        ],
        out_specs=[
            tall(inner),
            tall(inner),
            pl.BlockSpec((8, STEP), lambda i: (0, i)),
            tall(width),
        ],
        out_shape=[
            jax.ShapeDtypeStruct((rows, inner), F32),
            jax.ShapeDtypeStruct((rows, inner), F32),
            jax.ShapeDtypeStruct((8, rows), F32),
            jax.ShapeDtypeStruct((rows, width), BF16),
        ],
        compiler_params=pltpu.CompilerParams(
            dimension_semantics=("arbitrary",), vmem_limit_bytes=VMEM_LIMIT
        ),
        name="middle",
    )(u, rec, gate, st, pdx, sin, og, wo, prm)


def turn_kernel(
    inner_total, scan, gate, dgate, sums, upre_c, rec, prm,
    dscan, dgr, glow, adj, psx, fin, gain_grad,
    state, decay,
):
    inner = gate.shape[1]
    pairs = inner // LANES
    at = pl.program_id(0)

    @pl.when(at == 0)
    def _():
        state[...] = jnp.zeros_like(state)
        decay[...] = jnp.ones_like(decay)
        gain_grad[...] = jnp.zeros_like(gain_grad)

    head = sums[...]
    column = jnp.concatenate([head, jnp.zeros((LANES - 8, STEP), F32)], 0).T
    inv = lax.rsqrt(column[:, 0:1] / inner_total + EPSILON)
    cube = inv * inv * inv * (column[:, 1:2] / inner_total)
    raw = gate[...]
    sig = jax.nn.sigmoid(raw)
    sil = raw * sig
    y = scan[...]
    gated = y * sil
    unit = gated * inv
    d_gate = dgate[...]
    gain = prm[1:2, :]
    glow[...] = (unit * gain).astype(BF16)
    gain_grad[...] += jnp.broadcast_to(jnp.sum(d_gate * unit, 0, keepdims=True), gain_grad.shape)
    d_gated = inv * gain * d_gate - gated * cube
    d_scan = d_gated * sil
    dscan[...] = d_scan
    dgr[...] = (d_gated * y * (sig * (1.0 + raw * (1.0 - sig)))).astype(BF16)
    input_c = silu(upre_c[...])
    for i in reversed(range(SUB)):
        rows = slice(i * CHUNK, (i + 1) * CHUNK)
        record = rec[rows, :]
        entry = record[:, ENTRY : ENTRY + 1] * jnp.exp(record)
        adj[i] = state[...]
        psx[8 * i : 8 * i + 8, :] = decay[...]
        passed = spread(entry[CHUNK - 1 :, :], pairs)
        fed = (d_scan[rows] * spread(entry, pairs)).astype(BF16)
        state[...] = passed * state[...] + nn(input_c[rows].T.astype(BF16), fed)
        decay[...] = decay[...] * passed
    fin[...] = state[...]


def turn(scan, gate, dgate, sums, u, rec, prm, inner_total):
    rows, inner = gate.shape
    steps = rows // STEP
    chunks = rows // CHUNK
    state_size = LANES
    c_block = u.shape[1] // LANES - 1

    def whole(a):
        return pl.BlockSpec(a.shape, lambda i: (0,) * a.ndim)

    def tall(cols):
        return pl.BlockSpec((STEP, cols), lambda i: (steps - 1 - i, 0))

    return pl.pallas_call(
        functools.partial(turn_kernel, float(inner_total)),
        grid=(steps,),
        in_specs=[
            tall(inner),
            tall(inner),
            tall(inner),
            pl.BlockSpec((8, STEP), lambda i: (0, steps - 1 - i)),
            pl.BlockSpec((STEP, LANES), lambda i: (steps - 1 - i, c_block)),
            tall(LANES),
            whole(prm),
        ],
        out_specs=[
            tall(inner),
            tall(inner),
            tall(inner),
            pl.BlockSpec((SUB, state_size, inner), lambda i: (steps - 1 - i, 0, 0)),
            pl.BlockSpec((8 * SUB, inner), lambda i: (steps - 1 - i, 0)),
            pl.BlockSpec((state_size, inner), lambda i: (0, 0)),
            pl.BlockSpec((8, inner), lambda i: (0, 0)),
        ],
        out_shape=[
            jax.ShapeDtypeStruct((rows, inner), F32),
            jax.ShapeDtypeStruct((rows, inner), BF16),
            jax.ShapeDtypeStruct((rows, inner), BF16),
            jax.ShapeDtypeStruct((chunks, state_size, inner), F32),
            jax.ShapeDtypeStruct((8 * chunks, inner), F32),
            jax.ShapeDtypeStruct((state_size, inner), F32),
            jax.ShapeDtypeStruct((8, inner), F32),
        ],
        scratch_shapes=[pltpu.VMEM((state_size, inner), F32), pltpu.VMEM((8, inner), F32)],
        compiler_params=pltpu.CompilerParams(
            dimension_semantics=("arbitrary",), vmem_limit_bytes=VMEM_LIMIT
        ),
        name="turn",
    )(scan, gate, dgate, sums, u, rec, prm)


def back_kernel(
    u, rec, dscan, st, pdx, sin, adj, psx, ain, prm, dtp,
    dpre, dstep, skip_acc, head_acc,
):
    inner = dscan.shape[1]
    pairs = inner // LANES
    heads = 2 * pairs

    @pl.when(pl.program_id(0) == 0)
    def _():
        skip_acc[...] = jnp.zeros_like(skip_acc)
        head_acc[...] = jnp.zeros_like(head_acc)

    raw = u[...]
    sig = jax.nn.sigmoid(raw)
    act = raw * sig
    slope = sig * (1.0 + raw * (1.0 - sig))
    above = iota((CHUNK, CHUNK), 0) <= iota((CHUNK, CHUNK), 1)
    upper = above.astype(F32)
    lane = iota((CHUNK, LANES), 1)
    gather_heads = (iota((inner, LANES), 0) // (LANES // 2) == iota((inner, LANES), 1)).astype(BF16)
    nega = dtp[1:2, :]
    for i in range(SUB):
        rows = slice(i * CHUNK, (i + 1) * CHUNK)
        record = rec[rows, :]
        turned = record.T
        state = st[i] + pdx[8 * i : 8 * i + 1, :] * sin[...]
        state_low = state.astype(BF16)
        later = adj[i] + psx[8 * i : 8 * i + 1, :] * ain[...]
        later_low = later.astype(BF16)
        x = act[rows, :inner]
        b_wide = act[rows, inner : inner + LANES]
        c_wide = act[rows, inner + LANES :]
        input_b = b_wide.astype(BF16)
        input_c = c_wide.astype(BF16)
        dy = dscan[rows, :]
        scores = nt(input_b, input_c)
        barred = jnp.where(
            above & (record[:, SEG : SEG + 1] == turned[SEG : SEG + 1, :]), 0.0, NEGATIVE
        )
        step = pltpu.roll(record, LANES - 8, axis=1)
        z = pltpu.roll(record, LANES - RAW, axis=1)
        d_scores = jnp.zeros((CHUNK, CHUNK), F32)
        direct = jnp.zeros((CHUNK, LANES), F32)
        arrivals = []
        dxs = []
        for j in range(pairs):
            cols = slice(j * LANES, (j + 1) * LANES)
            x_sides = halves(x[:, cols].astype(BF16))
            dy_pair = dy[:, cols].astype(BF16)
            dy_sides = halves(dy_pair)
            total = None
            for k in range(2):
                h = 2 * j + k
                step_col = record[:, 8 + h : 9 + h]
                link = jnp.exp(turned[h : h + 1, :] - record[:, h : h + 1] + barred)
                d_link = nt(x_sides[k], dy_pair) * link
                d_scaled = d_link * step_col
                d_scores = d_scores + d_scaled
                flow = d_scaled * scores
                arrivals.append(jnp.sum(flow, 0, keepdims=True))
                given = jnp.sum(d_link * scores, 1, keepdims=True)
                direct = jnp.where(lane == h, given, direct)
                weight = (scores * link * step_col).astype(BF16)
                term = nn(weight, dy_sides[k])
                total = term if total is None else total + term
            dxs.append(total)
        dx = jnp.concatenate(dxs, 1)
        arrived = jnp.concatenate(arrivals + [jnp.zeros((CHUNK - heads, CHUNK), F32)], 0).T
        decay_in = record[:, ENTRY : ENTRY + 1] * jnp.exp(record)
        last = record[CHUNK - 1 :, :]
        tail_exp = record[:, TAIL : TAIL + 1] * jnp.exp(last - record)
        tail = tail_exp * step
        tail_wide = spread(jnp.where(lane < 8, tail, 0.0), pairs)
        fed_back = (dy * spread(decay_in, pairs)).astype(BF16)
        fed = (x * tail_wide).astype(BF16)
        from_state = nn(input_c, state_low)
        d_fed = nn(input_b, later_low)
        d_score_low = d_scores.astype(BF16)
        d_c = nt(fed_back, state_low) + nn(d_scores.T.astype(BF16), input_b)
        d_b = nt(fed, later_low) + nn(d_score_low, input_c)
        d_entry = nn((dy * from_state).astype(BF16), gather_heads)
        d_tail = nn((x * d_fed).astype(BF16), gather_heads)
        through = jnp.broadcast_to(jnp.sum(later * state, 0, keepdims=True), (16, inner))
        d_through = nn(through.astype(BF16), gather_heads)[0:1, :]
        dx = dx + d_fed * tail_wide + prm[0:1, :] * dy
        tail_flow = d_tail * tail
        d_cum = arrived - direct * step + d_entry * decay_in - tail_flow
        d_cum = jnp.where(lane < 8, d_cum, 0.0)
        d_last = jnp.sum(tail_flow, 0, keepdims=True) + decay_in[CHUNK - 1 :, :] * d_through
        d_rate = exact(upper, d_cum) + jnp.where(lane < 8, d_last, 0.0)
        d_step = direct + d_tail * tail_exp + nega * d_rate
        d_z = jnp.where(lane < 8, d_step * jax.nn.sigmoid(z), 0.0)
        dstep[rows, :] = d_z.astype(BF16)
        dpre[rows, :] = jnp.concatenate([dx, d_b, d_c], 1) * slope[rows]
        skip_acc[...] += jnp.broadcast_to(jnp.sum(dy * x, 0, keepdims=True), skip_acc.shape)
        head_acc[0:1, :] += jnp.sum(d_z, 0, keepdims=True)
        head_acc[1:2, :] += jnp.sum(
            jnp.where(lane < 8, d_rate * (nega * step), 0.0), 0, keepdims=True
        )


def back(u, rec, dscan, st, pdx, sin, adj, psx, ain, prm, dtp, group):
    rows, inner = dscan.shape
    steps = rows // STEP // GROUPS
    wide = u.shape[1]
    first = group * steps

    def whole(a):
        return pl.BlockSpec(a.shape, lambda i: (0,) * a.ndim)

    def tall(cols):
        return pl.BlockSpec((STEP, cols), lambda i: (first + i, 0))

    def out_tall(cols):
        return pl.BlockSpec((STEP, cols), lambda i: (i, 0))

    states = pl.BlockSpec((SUB,) + st.shape[1:], lambda i: (first + i, 0, 0))
    decays = pl.BlockSpec((8 * SUB, inner), lambda i: (first + i, 0))
    return pl.pallas_call(
        back_kernel,
        grid=(steps,),
        in_specs=[
            tall(wide), tall(LANES), tall(inner), states, decays, whole(sin),
            states, decays, whole(ain), whole(prm), whole(dtp),
        ],
        out_specs=[
            out_tall(wide),
            out_tall(LANES),
            pl.BlockSpec((8, inner), lambda i: (0, 0)),
            pl.BlockSpec((8, LANES), lambda i: (0, 0)),
        ],
        out_shape=[
            jax.ShapeDtypeStruct((steps * STEP, wide), F32),
            jax.ShapeDtypeStruct((steps * STEP, LANES), BF16),
            jax.ShapeDtypeStruct((8, inner), F32),
            jax.ShapeDtypeStruct((8, LANES), F32),
        ],
        compiler_params=pltpu.CompilerParams(
            dimension_semantics=("arbitrary",), vmem_limit_bytes=VMEM_LIMIT
        ),
        name="back",
    )(u, rec, dscan, st, pdx, sin, adj, psx, ain, prm, dtp)


def rear_kernel(
    dpre, rec, pre, dgr, dstep, follow, hid, w, cw,
    dproj, dnorm, conv_acc, gain_acc,
    buf, mbuf,
):
    wide = dpre.shape[1]
    inner = dgr.shape[1]

    @pl.when(pl.program_id(0) == 0)
    def _():
        buf[STEP : STEP + 8, :] = follow[:, :wide]
        mbuf[STEP : STEP + 8, :] = follow[:, wide:]
        conv_acc[...] = jnp.zeros_like(conv_acc)
        gain_acc[...] = jnp.zeros_like(gain_acc)

    @pl.when(pl.program_id(0) > 0)
    def _():
        buf[STEP : STEP + 8, :] = buf[0:8, :]
        mbuf[STEP : STEP + 8, :] = mbuf[0:8, :]

    grad = dpre[...]
    buf[0:STEP, :] = grad
    mbuf[0:STEP, :] = rec[...]
    value = pre[...]
    total = cw[3:4, :] * grad
    conv_acc[3:4, :] += jnp.sum(value * grad, 0, keepdims=True)
    conv_acc[4:5, :] += jnp.sum(grad, 0, keepdims=True)
    for shift in (1, 2, 3):
        mark = mbuf[shift : shift + STEP, :][:, M1 + shift - 1 : M1 + shift]
        moved = buf[shift : shift + STEP, :] * mark
        total = total + cw[3 - shift : 4 - shift, :] * moved
        conv_acc[3 - shift : 4 - shift, :] += jnp.sum(value * moved, 0, keepdims=True)
    dproj[:, :inner] = dgr[...]
    dproj[:, inner : inner + wide] = total.astype(BF16)
    dproj[:, inner + wide :] = dstep[...]
    grad_in = nt(dproj[...], w[...])
    dnorm[...] = grad_in.astype(BF16)
    unit = rms_unit(hid[...].astype(F32))
    gain_acc[...] += jnp.broadcast_to(jnp.sum(grad_in * unit, 0, keepdims=True), gain_acc.shape)


def rear(dpre, rec, pre, dgr, dstep, follow, hid, w, cw, group):
    rows, wide = dpre.shape
    steps = rows // STEP
    inner = dgr.shape[1]
    width, packed = w.shape
    first = group * steps

    def whole(a):
        return pl.BlockSpec(a.shape, lambda i: (0,) * a.ndim)

    def tall(cols):
        return pl.BlockSpec((STEP, cols), lambda i: (first + steps - 1 - i, 0))

    def own(cols):
        return pl.BlockSpec((STEP, cols), lambda i: (steps - 1 - i, 0))

    return pl.pallas_call(
        rear_kernel,
        grid=(steps,),
        in_specs=[
            own(wide), tall(LANES), tall(wide), tall(inner), own(LANES), whole(follow),
            tall(width), whole(w), whole(cw),
        ],
        out_specs=[
            own(packed),
            own(width),
            pl.BlockSpec((8, wide), lambda i: (0, 0)),
            pl.BlockSpec((8, width), lambda i: (0, 0)),
        ],
        out_shape=[
            jax.ShapeDtypeStruct((rows, packed), BF16),
            jax.ShapeDtypeStruct((rows, width), BF16),
            jax.ShapeDtypeStruct((8, wide), F32),
            jax.ShapeDtypeStruct((8, width), F32),
        ],
        scratch_shapes=[
            pltpu.VMEM((STEP + 8, wide), F32),
            pltpu.VMEM((STEP + 8, LANES), F32),
        ],
        compiler_params=pltpu.CompilerParams(
            dimension_semantics=("arbitrary",), vmem_limit_bytes=VMEM_LIMIT
        ),
        name="rear",
    )(dpre, rec, pre, dgr, dstep, follow, hid, w, cw)


def passed_along(value, axis, steps):
    count = lax.axis_size(axis)
    leading, last = (max(0, -steps), min(count, count - steps))
    return lax.ppermute(value, axis, [(source, source + steps) for source in range(leading, last)])


def chained(own, decay, axis, steps):
    entering = jnp.zeros_like(own)
    for turn_at in range(lax.axis_size(axis) - 1):
        leaving = own if turn_at == 0 else own + decay * entering
        entering = passed_along(leaving, axis, steps)
    return entering


def token_marks(segment, before):
    rows = segment.shape[0]
    joined = jnp.concatenate([before, segment])
    marks = [joined[3 - j : 3 - j + rows] == segment for j in (1, 2, 3)]
    blocks = segment.reshape(-1, CHUNK)
    previous = jnp.concatenate([before[2:], blocks[:-1, -1]])
    marks.append((blocks == previous[:, None]).reshape(-1))
    marks.append((blocks == blocks[:, -1:]).reshape(-1))
    marks.append(segment)
    table = jnp.stack([mark.astype(F32) for mark in marks], 1)
    return jnp.pad(table, ((0, 0), (M1, LANES - M1 - len(marks))))


def body(
    hidden, segments, out_grad, norm_gain, w_zx, w_dt, w_bc, conv_x_w, conv_x_b,
    conv_bc_w, conv_bc_b, dt_bias, a_log, skip_d, out_gain, w_out,
):
    _, rows, width = hidden.shape
    inner = w_zx.shape[2]
    heads = w_dt.shape[1]
    head_size = inner // heads
    state_size = w_bc.shape[2]
    wide = inner + 2 * state_size
    taps = conv_x_w.shape[0]
    owned = w_zx.shape[0]
    shards = ("fsdp", "ctx")
    hid = hidden[0]
    cot = out_grad[0]
    segment = segments[0]

    packed = jnp.concatenate(
        [
            w_zx.reshape(owned, 2 * inner),
            w_bc.reshape(owned, 2 * state_size),
            w_dt, w_dt, w_dt, w_dt,
            norm_gain[:, None],
            jnp.zeros((owned, LANES - 4 * heads - 1), BF16),
        ],
        1,
    )
    w_in = lax.all_gather(packed, shards, axis=0, tiled=True)
    wo = lax.all_gather(w_out.T, shards, axis=0, tiled=True)
    gain_at = 2 * inner + 2 * state_size + 4 * heads
    gain = w_in[:, gain_at].astype(F32)[None, :]

    edge, edge_segment = passed_along((hid[rows - EDGE :], segment[rows - 3 :]), "ctx", 1)
    tok = token_marks(segment, edge_segment)
    conv_rows = jnp.concatenate(
        [
            jnp.concatenate([conv_x_w, conv_bc_w.reshape(taps, -1)], 1),
            jnp.concatenate([conv_x_b, conv_bc_b.reshape(-1)])[None],
            jnp.zeros((8 - taps - 1, wide), F32),
        ],
        0,
    )
    spare = jnp.zeros((LANES - 4 * heads,), F32)
    rate = -jnp.exp(a_log)
    dtp = jnp.concatenate(
        [
            jnp.concatenate([dt_bias] * 4 + [spare])[None],
            jnp.concatenate([rate] * 4 + [spare])[None],
            jnp.zeros((6, LANES), F32),
        ],
        0,
    )
    prm = jnp.concatenate(
        [jnp.repeat(skip_d, head_size)[None], out_gain[None], jnp.zeros((6, inner), F32)], 0
    )

    normed, gate, pre, u, rec, st, pdx, state_end, decay_end = front(
        hid, edge, tok, w_in, gain, conv_rows, dtp, inner, wide
    )
    sin = chained(state_end, decay_end[:1], "ctx", 1)
    scan, dgate, sums, part = middle(u, rec, gate, st, pdx, sin, cot, wo, prm)
    sums = lax.psum(sums, "tp")
    out_sum = lax.psum(part, "tp")
    inner_total = inner * lax.axis_size("tp")
    dscan, dgr, glow, adj, psx, adj_start, out_gain_acc = turn(
        scan, gate, dgate, sums, u, rec, prm, inner_total
    )
    ain = chained(adj_start, decay_end[:1], "ctx", -1)
    inv_gate = lax.rsqrt(sums[0] / inner_total + EPSILON)[:, None]
    block_out = (hid.astype(F32) + inv_gate * out_sum.astype(F32)).astype(BF16)

    backs = []
    for group in range(GROUPS):
        backs.append(back(u, rec, dscan, st, pdx, sin, adj, psx, ain, prm, dtp, group))
    group_rows = rows // GROUPS
    heads_of = [
        jnp.concatenate([backs[g][0][:8], rec[g * group_rows : g * group_rows + 8]], 1)
        for g in range(GROUPS)
    ]
    follows = heads_of[1:] + [passed_along(heads_of[0], "ctx", -1)]
    rears = []
    d_normed = []
    for group in range(GROUPS):
        rears.append(
            rear(
                backs[group][0], rec, pre, dgr, backs[group][1], follows[group], hid, w_in,
                conv_rows, group,
            )
        )
        d_normed.append(lax.psum(rears[-1][1], "tp"))
    dproj = jnp.concatenate([r[0] for r in rears], 0)
    conv_acc = sum(r[2] for r in rears)
    gain_acc = sum(r[3][0] for r in rears)
    skip_acc = sum(b[2][0] for b in backs)
    head_acc = sum(b[3] for b in backs)

    contract_rows = (((0,), (0,)), ((), ()))
    w_grad = lax.dot_general(normed, dproj, contract_rows, preferred_element_type=F32)
    wo_grad = lax.dot_general(cot, glow, contract_rows, preferred_element_type=F32)
    w_grad = w_grad.at[:, gain_at].set(gain_acc)
    w_owned = lax.psum_scatter(w_grad, shards, scatter_dimension=0, tiled=True)
    wo_owned = lax.psum_scatter(wo_grad, shards, scatter_dimension=0, tiled=True)

    small = jnp.concatenate(
        [
            conv_acc[: taps + 1].reshape(-1),
            out_gain_acc[0],
            skip_acc,
            head_acc[:2].reshape(-1),
        ]
    )
    small = lax.psum(small, shards)
    conv_sum = small[: (taps + 1) * wide].reshape(taps + 1, wide)
    rest = small[(taps + 1) * wide :]
    shared = jnp.concatenate(
        [
            w_owned[:, 2 * inner : 2 * inner + 2 * state_size].reshape(-1),
            w_owned[:, gain_at],
            conv_sum[:, inner:].reshape(-1),
        ]
    )
    shared = lax.psum(shared, "tp")
    bc_size = owned * 2 * state_size
    bc_owned = shared[:bc_size].reshape(owned, 2, state_size)
    gain_owned = shared[bc_size : bc_size + owned]
    conv_bc = shared[bc_size + owned :].reshape(taps + 1, 2, state_size)

    tokens = hid.astype(F32)
    inv_rms = lax.rsqrt(jnp.mean(tokens * tokens, -1, keepdims=True) + EPSILON)
    grads = []
    for group in range(GROUPS):
        span = slice(group * group_rows, (group + 1) * group_rows)
        scaled = d_normed[group].astype(F32) * gain
        inv = inv_rms[span]
        cross = jnp.sum(scaled * tokens[span], -1, keepdims=True) / width
        grads.append(
            cot[span].astype(F32) + inv * scaled - tokens[span] * (inv * inv * inv * cross)
        )
    hidden_grad = jnp.concatenate(grads, 0)

    return (
        block_out[None],
        hidden_grad[None],
        gain_owned,
        w_owned[:, : 2 * inner].reshape(owned, 2, inner),
        w_owned[:, 2 * inner + 2 * state_size : 2 * inner + 2 * state_size + heads],
        bc_owned,
        conv_sum[:taps, :inner],
        conv_sum[taps, :inner],
        conv_bc[:taps],
        conv_bc[taps],
        rest[2 * inner : 2 * inner + heads],
        rest[2 * inner + LANES : 2 * inner + LANES + heads],
        jnp.sum(rest[inner : 2 * inner].reshape(heads, head_size), 1),
        rest[:inner],
        wo_owned.T,
    )


def solution(mesh):
    placed = (
        P("fsdp", "ctx", None),
        P("fsdp", "ctx"),
        P("fsdp", "ctx", None),
        P(("fsdp", "ctx")),
        P(("fsdp", "ctx"), None, "tp"),
        P(("fsdp", "ctx"), "tp"),
        P(("fsdp", "ctx"), None, None),
        P(None, "tp"),
        P("tp"),
        P(),
        P(),
        P("tp"),
        P("tp"),
        P("tp"),
        P("tp"),
        P("tp", ("fsdp", "ctx")),
    )
    return jax.shard_map(
        body,
        mesh=mesh,
        in_specs=placed,
        out_specs=(
            P("fsdp", "ctx", None),
            P("fsdp", "ctx", None),
            P(("fsdp", "ctx")),
            P(("fsdp", "ctx"), None, "tp"),
            P(("fsdp", "ctx"), "tp"),
            P(("fsdp", "ctx"), None, None),
            P(None, "tp"),
            P("tp"),
            P(),
            P(),
            P("tp"),
            P("tp"),
            P("tp"),
            P("tp"),
            P("tp", ("fsdp", "ctx")),
        ),
        check_vma=False,
    )
```

time: 1480 us -> 700 us (0.47)
  local copies, waits for them, and re-layouts: 318 us -> 37.9 us
  matrix products: 259 us -> 16 us
  other arithmetic: 181 us -> 33.9 us
  blocking collectives: 163 us -> 26 us
  Pallas kernels: 0 us -> 132 us
  waiting for transfers between devices: 512 us -> 420 us
    dot_general x127 -> x2, matrix products: 259 us -> 16 us  [the longest x1 10 us: body(): lax.dot_general(normed, dproj, contract_rows, preferred_element_type=F32)]
    pallas_call x0 -> x11, Pallas kernels: none -> 132 us  [the longest x4 47.1 us: back(): pl.pallas_call(back_kernel, grid=(steps,), in_specs=[tall(wide), tall(LAN...]
    dynamic_update_slice x40 -> x0, local copies, waits for them, and re-layouts: 123 us -> none  [piece_front(): lax.scan(jax.checkpoint(block_step), initial, stacked)]
    psum x2 -> x3, waiting for transfers between devices: 426 us -> 331 us  [the longest x1 284 us: body(): out_sum = lax.psum(part, 'tp')]
    psum x3 -> x1, blocking collectives: 102 us -> 26 us  [body(): small = lax.psum(small, shards)]
    another operation x71 -> x3, other arithmetic: 58.1 us -> 1.56 us
    squeeze x48 -> x0, local copies, waits for them, and re-layouts: 37.2 us -> none  [piece_front(): lax.scan(jax.checkpoint(block_step), initial, stacked)]
    all_gather x7 -> x0, blocking collectives: 36.6 us -> none  [the longest x1 9.9 us: body(): lax.all_gather(w_bc, ('fsdp', 'ctx'), axis=0, tiled=True)]
  transfers between devices with their start and end apart: 13 -> 12, of which waited for: 5 -> 8; matrix products, arithmetic and copies ran while one was open for 27% -> 9% of each run, Pallas kernels for 0% -> 12%
where the time goes in v1:
time: 700 us; the launch traced here: 691 us
  waiting for transfers between devices  420 us (60%)
  Pallas kernels  132 us (19%)
  local copies, waits for them, and re-layouts  37.9 us (5%)
  other arithmetic  33.9 us (5%)
  blocking collectives  26 us (4%)
  matrix products  16 us (2%)
  between operations  15.2 us (2%)
  starting transfers between devices  9.15 us (1%)
    psum x1, waiting for transfers between devices, body(): out_sum = lax.psum(part, 'tp')  284 us
    pallas_call x4, Pallas kernels, back(): pl.pallas_call(back_kernel, grid=(steps,), in_specs=[tall(wide), tall(LAN...  47.1 us
    reduce_scatter x1, waiting for transfers between devices, body(): lax.psum_scatter(wo_grad, shards, scatter_dimension=0, tiled=True)  40.2 us
    psum x1, waiting for transfers between devices, body(): sums = lax.psum(sums, 'tp')  34.1 us
    pallas_call x4, Pallas kernels, rear(): pl.pallas_call(rear_kernel, grid=(steps,), in_specs=[own(wide), tall(LANE...  30 us
    psum x1, blocking collectives, body(): small = lax.psum(small, shards)  26 us
    pallas_call x1, Pallas kernels, front(): pl.pallas_call(front_kernel, grid=(steps,), in_specs=[tall(width), whole(...  24.2 us
    reduce_scatter x1, waiting for transfers between devices, body(): w_owned = lax.psum_scatter(w_grad, shards, scatter_dimension=0, tiled=True)  24.2 us
  transfers between devices with their start and end apart: 12, of which 8 were waited for; matrix products, arithmetic and copies ran while one was open for 9% of the time, Pallas kernels for 12%

profile of v1, /device:TPU:0, one launch (start us, length us, event | category | flops | bytes accessed | tf_op | source)
XLA Modules:
  0.0 690.6 jit_solution(1929443173108600131)
XLA Ops:
  7.3 1.0 copy.82
  8.3 0.9 copy.88
  10.7 0.9 concatenate.58
  12.5 2.3 collective-permute-start
  15.5 1.3 collective-permute-start.1
  21.8 1.3 pad.6.tok
  23.1 22.6 %all-gather.3.cloned.1.call-done.w = bf16[1024,1408]{1,0:T(8,128)(2,1)} async-done(((bf16[128,1408]{1,0:T(8,128)(2,1)}), bf16[1024,1408]{1,0:T(8,128)(2,1)}) %all-gather.3.cloned.1.call-update) | async-done | bytes 2883600 | tf_op jit(solution)/shard_map/all_gather | solution.py:656
  45.7 1.8 convert_reduce_fusion
  48.1 24.2 %front.1 = (bf16[2048,1024]{1,0:T(8,128)(2,1)}, f32[2048,512]{1,0:T(8,128)}, f32[2048,768]{1,0:T(8,128)}, f32[2048,768]{1,0:T(8,128)}, f32[2048,128]{1,0:T(8,128...) custom-call(bf16[2048,1024]{1,0:T(8,128)(2,1)} %bitcast.89, ...), custom_call_target="tpu_custom_call" | custom-call | tf_op jit(solution)/shard_map/front/pallas_call | solution.py:144
  72.3 2.2 collective-permute-start.2
  76.6 16.5 %middle.1 = (f32[2048,512]{1,0:T(8,128)}, f32[2048,512]{1,0:T(8,128)}, f32[8,2048]{1,0:T(8,128)}, bf16[2048,1024]{1,0:T(8,128)(2,1)}) custom-call(f32[2048,768]{1,0:T(8,128)} %get-tuple-element.78.u.upre_c, f32[2048,128]{1,0:T(8,128)} %get-tuple-element.79.rec, f32[2048,512]{1,0:T(8,128)} %get-tuple-element.80.gate, f32[16,128,512]{2,1,0:T(8,128)} %get-tuple-element.81.st, ...), custom_call_target="tpu_custom_call" | custom-call | tf_op jit(solution)/shard_map/middle/pallas_call | solution.py:239
  93.2 34.1 %all-reduce.6.cloned.1.call-done.sums = f32[8,2048]{1,0:T(8,128)} async-done(((f32[8,2048]{1,0:T(8,128)}), f32[8,2048]{1,0:T(8,128)}) %all-reduce.6.cloned.1.call-update) | async-done | bytes 65552 | tf_op jit(solution)/shard_map/psum | solution.py:690
  127.3 14.1 %turn.1 = (f32[2048,512]{1,0:T(8,128)}, bf16[2048,512]{1,0:T(8,128)(2,1)}, bf16[2048,512]{1,0:T(8,128)(2,1)}, f32[16,128,512]{2,1,0:T(8,128)}, f32[128,512]{1,0:...) custom-call(f32[2048,512]{1,0:T(8,128)} %get-tuple-element.86.scan, f32[2048,512]{1,0:T(8,128)} %get-tuple-element.80.gate, ...), custom_call_target="tpu_custom_call" | custom-call | tf_op jit(solution)/shard_map/turn/pallas_call | solution.py:332
  141.4 1.3 collective-permute-start.3
  144.1 1.0 collective-permute-done.3.ain
  145.7 11.8 %back.4 = (f32[512,768]{1,0:T(8,128)}, bf16[512,128]{1,0:T(8,128)(2,1)}, f32[8,512]{1,0:T(8,128)}, f32[8,128]{1,0:T(8,128)}) custom-call(f32[2048,768]{1,0:T(8,128)} %get-tuple-element.78.u.upre_c, f32[2048,128]{1,0:T(8,128)} %get-tuple-element.79.rec, f32[2048,512]{1,0:T(8,128)} %get-tuple-element.88.dscan, f32[16,128,512]{2,1,0:T(8,128)} %get-tuple-element.81.st, ...), custom_call_target="tpu_custom_call" | custom-call | tf_op jit(solution)/shard_map/back/pallas_call | solution.py:489
  158.3 1.5 collective-permute-start.4
  159.7 11.8 %back.5 = (f32[512,768]{1,0:T(8,128)}, bf16[512,128]{1,0:T(8,128)(2,1)}, f32[8,512]{1,0:T(8,128)}, f32[8,128]{1,0:T(8,128)}) custom-call(f32[2048,768]{1,0:T(8,128)} %get-tuple-element.78.u.upre_c, f32[2048,128]{1,0:T(8,128)} %get-tuple-element.79.rec, f32[2048,512]{1,0:T(8,128)} %get-tuple-element.88.dscan, f32[16,128,512]{2,1,0:T(8,128)} %get-tuple-element.81.st, ...), custom_call_target="tpu_custom_call" | custom-call | tf_op jit(solution)/shard_map/back/pallas_call | solution.py:489
  172.2 11.8 %back.6 = (f32[512,768]{1,0:T(8,128)}, bf16[512,128]{1,0:T(8,128)(2,1)}, f32[8,512]{1,0:T(8,128)}, f32[8,128]{1,0:T(8,128)}) custom-call(f32[2048,768]{1,0:T(8,128)} %get-tuple-element.78.u.upre_c, f32[2048,128]{1,0:T(8,128)} %get-tuple-element.79.rec, f32[2048,512]{1,0:T(8,128)} %get-tuple-element.88.dscan, f32[16,128,512]{2,1,0:T(8,128)} %get-tuple-element.81.st, ...), custom_call_target="tpu_custom_call" | custom-call | tf_op jit(solution)/shard_map/back/pallas_call | solution.py:489
  184.8 11.8 %back.7 = (f32[512,768]{1,0:T(8,128)}, bf16[512,128]{1,0:T(8,128)(2,1)}, f32[8,512]{1,0:T(8,128)}, f32[8,128]{1,0:T(8,128)}) custom-call(f32[2048,768]{1,0:T(8,128)} %get-tuple-element.78.u.upre_c, f32[2048,128]{1,0:T(8,128)} %get-tuple-element.79.rec, f32[2048,512]{1,0:T(8,128)} %get-tuple-element.88.dscan, f32[16,128,512]{2,1,0:T(8,128)} %get-tuple-element.81.st, ...), custom_call_target="tpu_custom_call" | custom-call | tf_op jit(solution)/shard_map/back/pallas_call | solution.py:489
  198.5 7.6 %rear.4 = (bf16[512,1408]{1,0:T(8,128)(2,1)}, bf16[512,1024]{1,0:T(8,128)(2,1)}, f32[8,768]{1,0:T(8,128)}, f32[8,1024]{1,0:T(8,128)}) custom-call(f32[512,768]{1,0:T(8,128)} %get-tuple-element.92.dpre, f32[2048,128]{1,0:T(8,128)} %get-tuple-element.79.rec, f32[2048,768]{1,0:T(8,128)} %get-tuple-element.93.pre, bf16[2048,512]{1,0:T(8,128)(2,1)} %get-tuple-element.94.dgr, ...), custom_call_target="tpu_custom_call" | custom-call | tf_op jit(solution)/shard_map/rear/pallas_call | solution.py:572
  206.1 7.4 %rear.5 = (bf16[512,1408]{1,0:T(8,128)(2,1)}, bf16[512,1024]{1,0:T(8,128)(2,1)}, f32[8,768]{1,0:T(8,128)}, f32[8,1024]{1,0:T(8,128)}) custom-call(f32[512,768]{1,0:T(8,128)} %get-tuple-element.96.dpre, f32[2048,128]{1,0:T(8,128)} %get-tuple-element.79.rec, f32[2048,768]{1,0:T(8,128)} %get-tuple-element.93.pre, bf16[2048,512]{1,0:T(8,128)(2,1)} %get-tuple-element.94.dgr, ...), custom_call_target="tpu_custom_call" | custom-call | tf_op jit(solution)/shard_map/rear/pallas_call | solution.py:572
  213.5 7.4 %rear.6 = (bf16[512,1408]{1,0:T(8,128)(2,1)}, bf16[512,1024]{1,0:T(8,128)(2,1)}, f32[8,768]{1,0:T(8,128)}, f32[8,1024]{1,0:T(8,128)}) custom-call(f32[512,768]{1,0:T(8,128)} %get-tuple-element.99.dpre, f32[2048,128]{1,0:T(8,128)} %get-tuple-element.79.rec, f32[2048,768]{1,0:T(8,128)} %get-tuple-element.93.pre, bf16[2048,512]{1,0:T(8,128)(2,1)} %get-tuple-element.94.dgr, ...), custom_call_target="tpu_custom_call" | custom-call | tf_op jit(solution)/shard_map/rear/pallas_call | solution.py:572
  221.6 7.5 %rear.7 = (bf16[512,1408]{1,0:T(8,128)(2,1)}, bf16[512,1024]{1,0:T(8,128)(2,1)}, f32[8,768]{1,0:T(8,128)}, f32[8,1024]{1,0:T(8,128)}) custom-call(f32[512,768]{1,0:T(8,128)} %get-tuple-element.102.dpre, f32[2048,128]{1,0:T(8,128)} %get-tuple-element.79.rec, f32[2048,768]{1,0:T(8,128)} %get-tuple-element.93.pre, bf16[2048,512]{1,0:T(8,128)(2,1)} %get-tuple-element.94.dgr, ...), custom_call_target="tpu_custom_call" | custom-call | tf_op jit(solution)/shard_map/rear/pallas_call | solution.py:572
  230.2 10.0 %fusion = f32[1024,1408]{1,0:T(8,128)S(1)} fusion(bf16[2048,1024]{1,0:T(8,128)(2,1)} %get-tuple-element.106, bf16[512,1408]{1,0:T(8,128)(2,1)} %get-tuple-element.110, bf16[512,1408]{1,0:T(8,128)(2,1)} %get-tuple-element.109, bf16[512,1408]{1,0:T(8,128)(2,1)} %get-tuple-element.108, bf16[512,1408]{1,0:T(8,128)(2,1)S(1)} %copy-done.31), kind=kOutput, calls=%fused_computation.3 | convolution fusion | flops 5928648704 | bytes 15728640 | tf_op jit(solution)/shard_map/dot_general | solution.py:726
  240.2 2.5 copy-done.2
  243.6 2.2 scatter.4
  246.8 7.0 %bitcast_convert_fusion.1 = f32[2048,1024]{1,0:T(8,128)} fusion(bf16[1,2048,1024]{2,1,0:T(8,128)(2,1)} %param.18), kind=kLoop, calls=%fused_computation.92 | loop fusion | flops 2097152 | bytes 12582912 | tf_op jit(solution)/shard_map/convert_element_type | solution.py:698
  255.4 26.0 %psum.62 = f32[5120]{0:T(1024)S(1)} all-reduce(f32[5120]{0:T(1024)S(1)} %pad_maximum_fusion.5), channel_id=1, replica_groups=mesh['fsdp'=4,'ctx'=2,'tp'=4] {'fsdp','ctx'}, use_global_device_ids=true, to_apply=%region_13.14 | all-reduce | flops 5120 | bytes 40960 | tf_op jit(solution)/shard_map/psum | solution.py:740
  281.5 24.2 %reduce-scatter.3.cloned.1.call-done = f32[128,1408]{1,0:T(8,128)} async-done(((f32[1024,1408]{1,0:T(8,128)}), f32[128,1408]{1,0:T(8,128)}) %reduce-scatter.3.cloned.1.call-update) | async-done | bytes 720912 | tf_op jit(solution)/shard_map/reduce_scatter | solution.py:729
  305.7 0.9 slice_bitcast_fusion
  306.7 1.0 slice_reduce_fusion
  308.5 5.9 convolution_bitcast_fusion
  314.4 0.9 fusion.18
  318.3 284.0 %all-reduce.10.cloned.1.call-done = (bf16[2048,1024]{1,0:T(8,128)(2,1)}, bf16[512,1024]{1,0:T(8,128)(2,1)}, bf16[512,1024]{1,0:T(8,128)(2,1)}, bf16[512,1024]{1,0:T(8,128)(2,1)}, bf16[512,1024]{1,0:T(8,128)(2,1)}) async-done(((bf16[2048,1024]{1,0:T(8,128)(2,1)}, bf16[512,1024]{1,0:T(8,128)(2,1)}, bf16[512,1024]{1,0:T(8,128)(2,1)}, bf16[512,1024]{1,0:T(8,128)(2,1)}, bf16[512,1024]{1,0:T(8,128)(2,1)}), ...) | async-done | bytes 8388624 | tf_op jit(solution)/shard_map/psum | solution.py:691
  602.4 5.9 multiply_reduce_fusion.4
  608.3 1.2 copy-done.5
  609.5 3.5 multiply_reduce_fusion
  613.1 1.8 copy-done.1
  616.9 1.9 fusion.12
  618.9 3.9 maximum_bitcast_fusion
  622.8 1.2 reshape.323
  624.7 13.2 %all-reduce.8.cloned.1.call-done = f32[34176]{0:T(1024)} async-done(((f32[34176]{0:T(1024)}), f32[34176]{0:T(1024)}) %all-reduce.8.cloned.1.call-update) | async-done | bytes 136720 | tf_op jit(solution)/shard_map/psum | solution.py:750
  637.9 1.2 slice.339
  639.1 1.6 slice.342
  640.6 1.3 slice.345
  641.9 1.2 slice_bitcast_fusion.2
  643.2 40.2 %reduce-scatter.5.cloned.1.call-done = f32[128,512]{0,1:T(8,128)} async-done(((f32[1024,512]{0,1:T(8,128)}), f32[128,512]{0,1:T(8,128)}) %reduce-scatter.5.cloned.1.call-update) | async-done | bytes 262160 | tf_op jit(solution)/shard_map/reduce_scatter | solution.py:730
  (169 shorter events, 28.6 us)
Async XLA Ops:
  7.2 10.5 %copy-start.10 = (s32[1,2048]{1,0:T(1,128)S(1)}, s32[1,2048]{1,0:T(1,128)}, u32[]{:S(2)}) copy-start(s32[1,2048]{1,0:T(1,128)} %param.19) | copy-start | bytes 24580
  7.2 9.6 %copy-start.11 = (bf16[512,128]{1,0:T(8,128)(2,1)S(1)}, bf16[512,128]{1,0:T(8,128)(2,1)}, u32[]{:S(2)}) copy-start(bf16[512,128]{1,0:T(8,128)(2,1)} %param.33) | copy-start | bytes 393220
  7.2 10.8 %copy-start.28 = (f32[2,128]{1,0:T(2,128)S(1)}, f32[2,128]{1,0:T(2,128)}, u32[]{:S(2)}) copy-start(f32[2,128]{1,0:T(2,128)} %param.28) | copy-start | bytes 3076
  7.2 10.8 %copy-start.26 = (f32[512]{0:T(512)S(1)}, f32[512]{0:T(512)}, u32[]{:S(2)}) copy-start(f32[512]{0:T(512)} %param.26) | copy-start | bytes 6148
  7.2 10.8 %copy-start.25 = (f32[4,2,128]{2,1,0:T(2,128)S(1)}, f32[4,2,128]{2,1,0:T(2,128)}, u32[]{:S(2)}) copy-start(f32[4,2,128]{2,1,0:T(2,128)} %param.27) | copy-start | bytes 12292
  7.2 10.8 %copy-start.32 = (f32[8]{0:T(128)S(1)}, f32[8]{0:T(128)}, u32[]{:S(2)}) copy-start(f32[8]{0:T(128)} %param.30) | copy-start | bytes 100
  7.2 10.9 %copy-start.20 = (f32[8]{0:T(128)S(1)}, f32[8]{0:T(128)}, u32[]{:S(2)}) copy-start(f32[8]{0:T(128)} %param.29) | copy-start | bytes 100
  7.3 11.2 %copy-start.19 = (f32[4,512]{1,0:T(4,128)S(1)}, f32[4,512]{1,0:T(4,128)}, u32[]{:S(2)}) copy-start(f32[4,512]{1,0:T(4,128)} %param.25) | copy-start | bytes 24580
  7.3 38.4 %all-gather.3.cloned.1.call-start = ((), (), s32[]{:S(2)}) async-start(), calls=%async_computation.2 | async-start | bytes 3244032 | tf_op jit(solution)/shard_map/all_gather | solution.py:656
  11.6 63.7 %all-gather.5.cloned.1.call-start = ((), (), s32[]{:S(2)}) async-start(), calls=%async_computation.3 | async-start | bytes 1179648 | tf_op jit(solution)/shard_map/all_gather | solution.py:657
  12.5 35.0 %collective-permute-start = (bf16[16,1024]{1,0:T(8,128)(2,1)S(1)}, bf16[16,1024]{1,0:T(8,128)(2,1)S(1)}, u32[]{:S(2)}, u32[]{:S(2)}) collective-permute-start(bf16[16,1024]{1,0:T(8,128)(2,1)S(1)} %slice_bitcast_fusion.1), channel_id=1, source_target_pairs={{0,4},{1,5},{2,6},{3,7},{8,12},{9,13},{10,14},{11,15},{16,20},{17,... | collective-permute-start | bytes 98312 | tf_op jit(solution)/shard_map/ppermute | solution.py:605
  15.5 4.2 collective-permute-start.1
  17.6 109.6 %all-reduce.6.cloned.1.call-start = ((), (), s32[]{:S(2)}) async-start(), calls=%async_computation.4 | async-start | bytes 131072 | tf_op jit(solution)/shard_map/psum | solution.py:690
  47.5 0.6 copy-start.13
  48.1 26.5 %copy-start.29 = (f32[8]{0:T(128)S(1)}, f32[8]{0:T(128)}, u32[]{:S(2)}) copy-start(f32[8]{0:T(128)} %param.31) | copy-start | bytes 100
  48.1 26.6 %copy-start.27 = (f32[512]{0:T(512)S(1)}, f32[512]{0:T(512)}, u32[]{:S(2)}) copy-start(f32[512]{0:T(512)} %param.32) | copy-start | bytes 6148
  72.3 3.6 collective-permute-start.2
  75.9 0.7 copy-start.3
  93.1 212.6 %reduce-scatter.3.cloned.1.call-start = ((), (), s32[]{:S(2)}) async-start(), calls=%async_computation.5 | async-start | bytes 6488064 | tf_op jit(solution)/shard_map/reduce_scatter | solution.py:729
  141.4 3.6 collective-permute-start.3
  145.0 0.7 copy-start.4
  158.3 62.7 %collective-permute-start.4 = (f32[8,896]{1,0:T(8,128)S(1)}, f32[8,896]{1,0:T(8,128)S(1)}, u32[]{:S(2)}, u32[]{:S(2)}) collective-permute-start(f32[8,896]{1,0:T(8,128)S(1)} %pad_maximum_fusion.4), channel_id=1, source_target_pairs={{4,0},{5,1},{6,2},{7,3},{12,8},{13,9},{14,10},{15,11},{20,16},{21,... | collective-permute-start | bytes 86024 | tf_op jit(solution)/shard_map/ppermute | solution.py:605
  221.6 8.6 %copy-start.31 = (bf16[512,1408]{1,0:T(8,128)(2,1)S(1)}, bf16[512,1408]{1,0:T(8,128)(2,1)}, u32[]{:S(2)}) copy-start(bf16[512,1408]{1,0:T(8,128)(2,1)} %get-tuple-element.107) | copy-start | bytes 4325380
  240.2 2.5 copy-start.2
  245.8 356.5 %all-reduce.10.cloned.1.call-start = ((), (), s32[]{:S(2)}) async-start(), calls=%async_computation.8 | async-start | bytes 16777216 | tf_op jit(solution)/shard_map/psum | solution.py:691
  246.4 8.1 %copy-start.21 = (f32[8,128]{1,0:T(8,128)S(1)}, f32[8,128]{1,0:T(8,128)}, u32[]{:S(2)}) copy-start(f32[8,128]{1,0:T(8,128)} %get-tuple-element.124) | copy-start | bytes 12292
  246.4 8.1 %copy-start.22 = (f32[8,128]{1,0:T(8,128)S(1)}, f32[8,128]{1,0:T(8,128)}, u32[]{:S(2)}) copy-start(f32[8,128]{1,0:T(8,128)} %get-tuple-element.125) | copy-start | bytes 12292
  246.5 8.1 %copy-start.23 = (f32[8,128]{1,0:T(8,128)S(1)}, f32[8,128]{1,0:T(8,128)}, u32[]{:S(2)}) copy-start(f32[8,128]{1,0:T(8,128)} %get-tuple-element.126) | copy-start | bytes 12292
  246.5 8.1 %copy-start.24 = (f32[8,128]{1,0:T(8,128)S(1)}, f32[8,128]{1,0:T(8,128)}, u32[]{:S(2)}) copy-start(f32[8,128]{1,0:T(8,128)} %get-tuple-element.127) | copy-start | bytes 12292
  246.5 8.9 %copy-start.15 = (f32[8,768]{1,0:T(8,128)S(1)}, f32[8,768]{1,0:T(8,128)}, u32[]{:S(2)}) copy-start(f32[8,768]{1,0:T(8,128)} %get-tuple-element.115) | copy-start | bytes 73732
  246.5 8.9 %copy-start.16 = (f32[8,768]{1,0:T(8,128)S(1)}, f32[8,768]{1,0:T(8,128)}, u32[]{:S(2)}) copy-start(f32[8,768]{1,0:T(8,128)} %get-tuple-element.116) | copy-start | bytes 73732
  246.5 8.9 %copy-start.17 = (f32[8,768]{1,0:T(8,128)S(1)}, f32[8,768]{1,0:T(8,128)}, u32[]{:S(2)}) copy-start(f32[8,768]{1,0:T(8,128)} %get-tuple-element.117) | copy-start | bytes 73732
  246.5 8.9 %copy-start.18 = (f32[8,768]{1,0:T(8,128)S(1)}, f32[8,768]{1,0:T(8,128)}, u32[]{:S(2)}) copy-start(f32[8,768]{1,0:T(8,128)} %get-tuple-element.118) | copy-start | bytes 73732
  246.5 62.0 %copy-start.30 = (bf16[2048,512]{1,0:T(8,128)(2,1)S(1)}, bf16[2048,512]{1,0:T(8,128)(2,1)}, u32[]{:S(2)}) copy-start(bf16[2048,512]{1,0:T(8,128)(2,1)} %get-tuple-element.128) | copy-start | bytes 6291460
  246.5 391.4 %all-reduce.8.cloned.1.call-start = ((), (), s32[]{:S(2)}) async-start(), calls=%async_computation.6 | async-start | bytes 278528 | tf_op jit(solution)/shard_map/psum | solution.py:750
  308.4 374.9 %reduce-scatter.5.cloned.1.call-start = ((), (), s32[]{:S(2)}) async-start(), calls=%async_computation.7 | async-start | bytes 2359296 | tf_op jit(solution)/shard_map/reduce_scatter | solution.py:730
  314.4 287.9 %copy-start.12 = (f32[1024]{0:T(1024)S(1)}, f32[1024]{0:T(1024)}, u32[]{:S(2)}) copy-start(f32[1024]{0:T(1024)} %convert_reduce_fusion) | copy-start | bytes 12292
  602.4 6.0 copy-start
  602.4 7.2 %copy-start.5 = (bf16[2048,1024]{1,0:T(8,128)(2,1)S(1)}, bf16[2048,1024]{1,0:T(8,128)(2,1)}, u32[]{:S(2)}) copy-start(bf16[2048,1024]{1,0:T(8,128)(2,1)} %get-tuple-element.193) | copy-start | bytes 12582916
  602.4 10.7 %slice-start = ((s8[8388608]{0:T(1024)(128)(4,1)}), s8[4194304]{0:T(1024)(128)(4,1)S(1)}, s32[]{:S(2)}) async-start(s8[8388608]{0:T(1024)(128)(4,1)} %bitcast.94), calls=%async_computation.9 | async-start | bytes 8388608
  609.5 3.6 slice-start.1
  609.5 5.3 copy-start.1
  609.5 5.6 copy-start.6
  615.1 1.2 copy-start.7
  615.1 1.5 copy-start.8
  615.1 1.9 copy-start.9
  618.9 3.9 slice-start.2
  622.8 1.2 slice-start.3
  (1 other events, 0.6 us)
Sparse Core Ops, SparseCore 0:
  11.8 33.9 all-gather.2
  48.2 23.5 all-gather.4
  93.2 33.9 all-reduce.5
  246.0 59.6 reduce-scatter.2
  308.6 293.6 all-reduce.9
  604.5 33.3 all-reduce.7
  642.1 41.2 reduce-scatter.4

commit v2 on v1

--- a/solution.py
+++ b/solution.py
@@ -40,6 +40,22 @@
     )
 
 
+def lasts(microseconds):
+    return pl.CostEstimate(
+        flops=0, bytes_accessed=int(microseconds * 3.69e6), transcendentals=0
+    )
+
+
+ANYWHERE = pl.BlockSpec(memory_space=pl.ANY)
+
+
+def ordered(kernel, inputs, after):
+    def run(*refs):
+        kernel(*refs[:inputs], *refs[inputs + after :])
+
+    return run
+
+
 def iota(shape, dim):
     return lax.broadcasted_iota(jnp.int32, shape, dim)
 
@@ -70,10 +86,11 @@
 
 
 def front_kernel(
-    hid, edge, tok, w, gain, cw, dtp,
-    normed, gate, pre_out, u_out, rec, st, pdx, fin, pdfin,
-    buf, state, decay,
+    gain_lane, starts, hid, edge, tok, cw, dtp, *refs
 ):
+    (normed, gate, pre_out, u_out, rec, st, pdx, fin, pdfin, w, gain_out,
+     buf, state, decay) = refs[-14:]
+    shards = refs[:-14]
     inner = gate.shape[1]
     wide = pre_out.shape[1]
     pairs = inner // LANES
@@ -81,7 +98,15 @@
 
     @pl.when(at == 0)
     def _():
-        edge_low = (rms_unit(edge[...].astype(F32)) * gain[...]).astype(BF16)
+        for k, shard in enumerate(shards):
+            size = shard.shape[0]
+            w[pl.ds(pl.multiple_of(starts[k], 16), size), :] = shard[...]
+        for k in range(w.shape[0] // LANES):
+            tile = w[k * LANES : (k + 1) * LANES, inner + wide :].astype(F32).T
+            gain_out[:, k * LANES : (k + 1) * LANES] = jnp.broadcast_to(
+                tile[gain_lane : gain_lane + 1, :], (8, LANES)
+            )
+        edge_low = (rms_unit(edge[...].astype(F32)) * gain_out[0:1, :]).astype(BF16)
         edge_pre = nn(edge_low, w[:, inner : inner + wide])
         buf[0:8, :] = edge_pre[EDGE - 8 :, :]
         state[...] = jnp.zeros_like(state)
@@ -91,7 +116,7 @@
     def _():
         buf[0:8, :] = buf[STEP : STEP + 8, :]
 
-    low = (rms_unit(hid[...].astype(F32)) * gain[...]).astype(BF16)
+    low = (rms_unit(hid[...].astype(F32)) * gain_out[0:1, :]).astype(BF16)
     normed[...] = low
     gate[...] = nn(low, w[:, :inner])
     pre = nn(low, w[:, inner : inner + wide])
@@ -129,8 +154,9 @@
     pdfin[...] = decay[...]
 
 
-def front(hidden, edge, tok, w, gain, cw, dtp, inner, wide):
+def front(hidden, edge, tok, shards, starts, gain_lane, cw, dtp, inner, wide):
     rows, width = hidden.shape
+    packed = shards[0].shape[1]
     steps = rows // STEP
     state_size = LANES
 
@@ -142,9 +168,17 @@
 
     chunks = rows // CHUNK
     return pl.pallas_call(
-        front_kernel,
+        functools.partial(front_kernel, gain_lane),
         grid=(steps,),
-        in_specs=[tall(width), whole(edge), tall(LANES), whole(w), whole(gain), whole(cw), whole(dtp)],
+        in_specs=[
+            pl.BlockSpec(memory_space=pltpu.SMEM),
+            tall(width),
+            whole(edge),
+            tall(LANES),
+            whole(cw),
+            whole(dtp),
+        ]
+        + [whole(shard) for shard in shards],
         out_specs=[
             tall(width),
             tall(inner),
@@ -155,6 +189,8 @@
             pl.BlockSpec((8 * SUB, inner), lambda i: (i, 0)),
             pl.BlockSpec((state_size, inner), lambda i: (0, 0)),
             pl.BlockSpec((8, inner), lambda i: (0, 0)),
+            pl.BlockSpec((width, packed), lambda i: (0, 0)),
+            pl.BlockSpec((8, width), lambda i: (0, 0)),
         ],
         out_shape=[
             jax.ShapeDtypeStruct((rows, width), BF16),
@@ -166,6 +202,8 @@
             jax.ShapeDtypeStruct((8 * chunks, inner), F32),
             jax.ShapeDtypeStruct((state_size, inner), F32),
             jax.ShapeDtypeStruct((8, inner), F32),
+            jax.ShapeDtypeStruct((width, packed), BF16),
+            jax.ShapeDtypeStruct((8, width), F32),
         ],
         scratch_shapes=[
             pltpu.VMEM((STEP + 8, wide), F32),
@@ -175,13 +213,14 @@
         compiler_params=pltpu.CompilerParams(
             dimension_semantics=("arbitrary",), vmem_limit_bytes=VMEM_LIMIT
         ),
+        cost_estimate=lasts(1),
         name="front",
-    )(hidden, edge, tok, w, gain, cw, dtp)
+    )(starts, hidden, edge, tok, cw, dtp, *shards)
 
 
 def middle_kernel(
     u, rec, gate, st, pdx, sin, og, wo, prm,
-    scan, dgate, sums, part,
+    scan, dgate, sums, part_first, part_second,
 ):
     inner = gate.shape[1]
     pairs = inner // LANES
@@ -223,55 +262,73 @@
     lane = iota((STEP, LANES), 1)
     both = jnp.where(lane == 0, squares, jnp.where(lane == 1, crosses, 0.0))
     sums[...] = both.T[0:8, :]
-    part[...] = nt(scaled.astype(BF16), wo[...]).astype(BF16)
-
-
-def middle(u, rec, gate, st, pdx, sin, og, wo, prm):
+    part = nt(scaled.astype(BF16), wo[...]).astype(BF16)
+    early = pl.program_id(0) < pl.num_programs(0) // 2
+
+    @pl.when(early)
+    def _():
+        part_first[...] = part
+
+    @pl.when(jnp.logical_not(early))
+    def _():
+        part_second[...] = part
+
+
+def middle(u, rec, gate, st, pdx, sin, og, wo, prm, half):
     rows, inner = gate.shape
     width = og.shape[1]
+    rows = rows // 2
+    steps = rows // STEP
+    first = half * steps
 
     def whole(a):
         return pl.BlockSpec(a.shape, lambda i: (0,) * a.ndim)
 
     def tall(cols):
+        return pl.BlockSpec((STEP, cols), lambda i: (first + i, 0))
+
+    def own(cols):
         return pl.BlockSpec((STEP, cols), lambda i: (i, 0))
 
     return pl.pallas_call(
         middle_kernel,
-        grid=(rows // STEP,),
+        grid=(steps,),
         in_specs=[
             tall(u.shape[1]),
             tall(LANES),
             tall(inner),
-            pl.BlockSpec((SUB,) + st.shape[1:], lambda i: (i, 0, 0)),
-            pl.BlockSpec((8 * SUB, inner), lambda i: (i, 0)),
+            pl.BlockSpec((SUB,) + st.shape[1:], lambda i: (first + i, 0, 0)),
+            pl.BlockSpec((8 * SUB, inner), lambda i: (first + i, 0)),
             whole(sin),
             tall(width),
             whole(wo),
             whole(prm),
         ],
         out_specs=[
-            tall(inner),
-            tall(inner),
+            own(inner),
+            own(inner),
             pl.BlockSpec((8, STEP), lambda i: (0, i)),
-            tall(width),
+            pl.BlockSpec((STEP, width), lambda i: (jnp.minimum(i, steps // 2 - 1), 0)),
+            pl.BlockSpec((STEP, width), lambda i: (jnp.maximum(i - steps // 2, 0), 0)),
         ],
         out_shape=[
             jax.ShapeDtypeStruct((rows, inner), F32),
             jax.ShapeDtypeStruct((rows, inner), F32),
             jax.ShapeDtypeStruct((8, rows), F32),
-            jax.ShapeDtypeStruct((rows, width), BF16),
+            jax.ShapeDtypeStruct((rows // 2, width), BF16),
+            jax.ShapeDtypeStruct((rows // 2, width), BF16),
         ],
         compiler_params=pltpu.CompilerParams(
             dimension_semantics=("arbitrary",), vmem_limit_bytes=VMEM_LIMIT
         ),
+        cost_estimate=lasts(1),
         name="middle",
     )(u, rec, gate, st, pdx, sin, og, wo, prm)
 
 
 def turn_kernel(
-    inner_total, scan, gate, dgate, sums, upre_c, rec, prm,
-    dscan, dgr, glow, adj, psx, fin, gain_grad,
+    inner_total, scan, gate, dgate, sums, upre_c, rec, prm, fin_before, decay_before,
+    dscan, dgr, glow, adj, psx, fin, gain_grad, decay_end,
     state, decay,
 ):
     inner = gate.shape[1]
@@ -280,8 +337,8 @@
 
     @pl.when(at == 0)
     def _():
-        state[...] = jnp.zeros_like(state)
-        decay[...] = jnp.ones_like(decay)
+        state[...] = fin_before[...]
+        decay[...] = decay_before[...]
         gain_grad[...] = jnp.zeros_like(gain_grad)
 
     head = sums[...]
@@ -314,12 +371,14 @@
         state[...] = passed * state[...] + nn(input_c[rows].T.astype(BF16), fed)
         decay[...] = decay[...] * passed
     fin[...] = state[...]
-
-
-def turn(scan, gate, dgate, sums, u, rec, prm, inner_total):
-    rows, inner = gate.shape
+    decay_end[...] = decay[...]
+
+
+def turn(scan, gate, dgate, sums, u, rec, prm, fin_before, decay_before, inner_total, half):
+    rows, inner = scan.shape
     steps = rows // STEP
     chunks = rows // CHUNK
+    first = half * steps
     state_size = LANES
     c_block = u.shape[1] // LANES - 1
 
@@ -327,27 +386,33 @@
         return pl.BlockSpec(a.shape, lambda i: (0,) * a.ndim)
 
     def tall(cols):
+        return pl.BlockSpec((STEP, cols), lambda i: (first + steps - 1 - i, 0))
+
+    def own(cols):
         return pl.BlockSpec((STEP, cols), lambda i: (steps - 1 - i, 0))
 
     return pl.pallas_call(
         functools.partial(turn_kernel, float(inner_total)),
         grid=(steps,),
         in_specs=[
+            own(inner),
             tall(inner),
-            tall(inner),
-            tall(inner),
+            own(inner),
             pl.BlockSpec((8, STEP), lambda i: (0, steps - 1 - i)),
-            pl.BlockSpec((STEP, LANES), lambda i: (steps - 1 - i, c_block)),
+            pl.BlockSpec((STEP, LANES), lambda i: (first + steps - 1 - i, c_block)),
             tall(LANES),
             whole(prm),
+            whole(fin_before),
+            whole(decay_before),
         ],
         out_specs=[
-            tall(inner),
-            tall(inner),
-            tall(inner),
+            own(inner),
+            own(inner),
+            own(inner),
             pl.BlockSpec((SUB, state_size, inner), lambda i: (steps - 1 - i, 0, 0)),
             pl.BlockSpec((8 * SUB, inner), lambda i: (steps - 1 - i, 0)),
             pl.BlockSpec((state_size, inner), lambda i: (0, 0)),
+            pl.BlockSpec((8, inner), lambda i: (0, 0)),
             pl.BlockSpec((8, inner), lambda i: (0, 0)),
         ],
         out_shape=[
@@ -358,13 +423,15 @@
             jax.ShapeDtypeStruct((8 * chunks, inner), F32),
             jax.ShapeDtypeStruct((state_size, inner), F32),
             jax.ShapeDtypeStruct((8, inner), F32),
+            jax.ShapeDtypeStruct((8, inner), F32),
         ],
         scratch_shapes=[pltpu.VMEM((state_size, inner), F32), pltpu.VMEM((8, inner), F32)],
         compiler_params=pltpu.CompilerParams(
             dimension_semantics=("arbitrary",), vmem_limit_bytes=VMEM_LIMIT
         ),
+        cost_estimate=lasts(1),
         name="turn",
-    )(scan, gate, dgate, sums, u, rec, prm)
+    )(scan, gate, dgate, sums, u, rec, prm, fin_before, decay_before)
 
 
 def back_kernel(
@@ -469,11 +536,12 @@
         )
 
 
-def back(u, rec, dscan, st, pdx, sin, adj, psx, ain, prm, dtp, group):
-    rows, inner = dscan.shape
+def back(u, rec, dscan, st, pdx, sin, adj, psx, ain, prm, dtp, after, group):
+    rows, wide = u.shape
+    inner = dscan.shape[1]
     steps = rows // STEP // GROUPS
-    wide = u.shape[1]
     first = group * steps
+    in_half = group % (GROUPS // 2) * steps
 
     def whole(a):
         return pl.BlockSpec(a.shape, lambda i: (0,) * a.ndim)
@@ -484,15 +552,29 @@
     def out_tall(cols):
         return pl.BlockSpec((STEP, cols), lambda i: (i, 0))
 
-    states = pl.BlockSpec((SUB,) + st.shape[1:], lambda i: (first + i, 0, 0))
-    decays = pl.BlockSpec((8 * SUB, inner), lambda i: (first + i, 0))
+    def states(at):
+        return pl.BlockSpec((SUB,) + st.shape[1:], lambda i: (at + i, 0, 0))
+
+    def decays(at):
+        return pl.BlockSpec((8 * SUB, inner), lambda i: (at + i, 0))
+
     return pl.pallas_call(
-        back_kernel,
+        ordered(back_kernel, 11, len(after)),
         grid=(steps,),
         in_specs=[
-            tall(wide), tall(LANES), tall(inner), states, decays, whole(sin),
-            states, decays, whole(ain), whole(prm), whole(dtp),
-        ],
+            tall(wide),
+            tall(LANES),
+            pl.BlockSpec((STEP, inner), lambda i: (in_half + i, 0)),
+            states(first),
+            decays(first),
+            whole(sin),
+            states(in_half),
+            decays(in_half),
+            whole(ain),
+            whole(prm),
+            whole(dtp),
+        ]
+        + [ANYWHERE] * len(after),
         out_specs=[
             out_tall(wide),
             out_tall(LANES),
@@ -508,12 +590,13 @@
         compiler_params=pltpu.CompilerParams(
             dimension_semantics=("arbitrary",), vmem_limit_bytes=VMEM_LIMIT
         ),
+        cost_estimate=lasts(1),
         name="back",
-    )(u, rec, dscan, st, pdx, sin, adj, psx, ain, prm, dtp)
+    )(u, rec, dscan, st, pdx, sin, adj, psx, ain, prm, dtp, *after)
 
 
 def rear_kernel(
-    dpre, rec, pre, dgr, dstep, follow, hid, w, cw,
+    dpre, rec, pre, dgr, dstep, follow, hid, w, cw, filled,
     dproj, dnorm, conv_acc, gain_acc,
     buf, mbuf,
 ):
@@ -553,8 +636,9 @@
     gain_acc[...] += jnp.broadcast_to(jnp.sum(grad_in * unit, 0, keepdims=True), gain_acc.shape)
 
 
-def rear(dpre, rec, pre, dgr, dstep, follow, hid, w, cw, group):
+def rear(dpre, rec, pre, dgr, dstep, follow, hid, w, cw, filled, after, group):
     rows, wide = dpre.shape
+    in_half = group % (GROUPS // 2) * (rows // STEP)
     steps = rows // STEP
     inner = dgr.shape[1]
     width, packed = w.shape
@@ -570,20 +654,29 @@
         return pl.BlockSpec((STEP, cols), lambda i: (steps - 1 - i, 0))
 
     return pl.pallas_call(
-        rear_kernel,
+        ordered(rear_kernel, 10, len(after)),
         grid=(steps,),
         in_specs=[
-            own(wide), tall(LANES), tall(wide), tall(inner), own(LANES), whole(follow),
-            tall(width), whole(w), whole(cw),
-        ],
+            own(wide),
+            tall(LANES),
+            tall(wide),
+            pl.BlockSpec((STEP, inner), lambda i: (in_half + steps - 1 - i, 0)),
+            own(LANES),
+            whole(follow),
+            tall(width),
+            whole(w),
+            whole(cw),
+            ANYWHERE,
+        ]
+        + [ANYWHERE] * len(after),
         out_specs=[
-            own(packed),
+            tall(packed),
             own(width),
             pl.BlockSpec((8, wide), lambda i: (0, 0)),
             pl.BlockSpec((8, width), lambda i: (0, 0)),
         ],
         out_shape=[
-            jax.ShapeDtypeStruct((rows, packed), BF16),
+            jax.ShapeDtypeStruct((pre.shape[0], packed), BF16),
             jax.ShapeDtypeStruct((rows, width), BF16),
             jax.ShapeDtypeStruct((8, wide), F32),
             jax.ShapeDtypeStruct((8, width), F32),
@@ -595,8 +688,53 @@
         compiler_params=pltpu.CompilerParams(
             dimension_semantics=("arbitrary",), vmem_limit_bytes=VMEM_LIMIT
         ),
+        cost_estimate=lasts(1),
+        input_output_aliases={9: 0} if group else {},
         name="rear",
-    )(dpre, rec, pre, dgr, dstep, follow, hid, w, cw)
+    )(dpre, rec, pre, dgr, dstep, follow, hid, w, cw, filled, *after)
+
+
+def settle_kernel(inner_total, hid, sums, given, held, outer, filled, out):
+    column = jnp.concatenate([sums[...], jnp.zeros((LANES - 8, STEP), F32)], 0).T
+    inv = lax.rsqrt(column[:, 0:1] / inner_total + EPSILON)
+    total = jnp.where(outer[0:1, 0:1] > 0.0, given[...].astype(F32), held[...].astype(F32))
+    out[...] = (hid[...].astype(F32) + inv * total).astype(BF16)
+
+
+def finish_kernel(hid, cot, gain, given, held, outer, filled, out):
+    x = hid[...].astype(F32)
+    inv = lax.rsqrt(jnp.mean(x * x, -1, keepdims=True) + EPSILON)
+    total = jnp.where(outer[0:1, 0:1] > 0.0, given[...].astype(F32), held[...].astype(F32))
+    scaled = total * gain[0:1, :]
+    cross = jnp.mean(scaled * x, -1, keepdims=True)
+    out[...] = cot[...].astype(F32) + inv * scaled - x * (inv * inv * inv * cross)
+
+
+def by_group(kernel, out_like, dtype, group, fresh, operands, filled, after, name):
+    rows, width = out_like.shape
+    steps = rows // GROUPS // STEP
+    first = group * steps
+    in_half = group % (GROUPS // 2) * steps
+    specs = {
+        "all": lambda a: pl.BlockSpec((STEP, a.shape[1]), lambda i: (first + i, 0)),
+        "group": lambda a: pl.BlockSpec((STEP, a.shape[1]), lambda i: (i, 0)),
+        "half": lambda a: pl.BlockSpec((8, STEP), lambda i: (0, in_half + i)),
+        "whole": lambda a: pl.BlockSpec(a.shape, lambda i: (0, 0)),
+    }
+    count = len(operands) + 1
+    return pl.pallas_call(
+        ordered(kernel, count, len(after)),
+        grid=(steps,),
+        in_specs=[specs[kind](a) for a, kind in operands] + [ANYWHERE] * (1 + len(after)),
+        out_specs=pl.BlockSpec((STEP, width), lambda i: (first + i, 0)),
+        out_shape=jax.ShapeDtypeStruct((rows, width), dtype),
+        input_output_aliases={} if fresh else {count - 1: 0},
+        compiler_params=pltpu.CompilerParams(
+            dimension_semantics=("arbitrary",), vmem_limit_bytes=VMEM_LIMIT
+        ),
+        cost_estimate=lasts(1),
+        name=name,
+    )(*[a for a, _ in operands], filled, *after)
 
 
 def passed_along(value, axis, steps):
@@ -611,6 +749,81 @@
         leaving = own if turn_at == 0 else own + decay * entering
         entering = passed_along(leaving, axis, steps)
     return entering
+
+
+def butterfly_sum(value, axis):
+    bit = 1
+    while bit < lax.axis_size(axis):
+        pairs = [(i, i ^ bit) for i in range(lax.axis_size(axis))]
+        value = value + lax.ppermute(value, axis, pairs)
+        bit *= 2
+    return value
+
+
+def join_kernel(a, b, out):
+    out[...] = (a[...].astype(F32) + b[...].astype(F32)).astype(out.dtype)
+
+
+def join(a, b, after):
+    rows, width = a.shape
+    spec = pl.BlockSpec((STEP, width), lambda i: (i, 0))
+    return pl.pallas_call(
+        ordered(join_kernel, 2, len(after)),
+        grid=(rows // STEP,),
+        in_specs=[spec, spec] + [ANYWHERE] * len(after),
+        out_specs=spec,
+        out_shape=jax.ShapeDtypeStruct(a.shape, a.dtype),
+        compiler_params=pltpu.CompilerParams(
+            dimension_semantics=("arbitrary",), vmem_limit_bytes=VMEM_LIMIT
+        ),
+        cost_estimate=lasts(1),
+        name="join",
+    )(a, b, *after)
+
+
+class LineSum:
+    def __init__(self, value, axis):
+        self.axis = axis
+        self.short = lax.axis_size(axis) != 4
+        if self.short:
+            self.near = self.across = self.given = lax.psum(value, axis)
+        else:
+            self.own = value
+            self.come = lax.ppermute(value, axis, [(0, 1), (3, 2)])
+
+    def inwards(self, after=()):
+        if not self.short:
+            self.near = join(self.own, self.come, after)
+            self.come = lax.ppermute(self.near, self.axis, [(1, 2), (2, 1)])
+
+    def middle(self, after=()):
+        if not self.short:
+            self.across = join(self.near, self.come, after)
+            self.given = lax.ppermute(self.across, self.axis, [(1, 0), (2, 3)])
+
+
+def gathered_shards(own):
+    rows = own.shape[0]
+    if lax.axis_size("fsdp") != 4 or lax.axis_size("ctx") != 2:
+        return [lax.all_gather(own, ("fsdp", "ctx"), axis=0, tiled=True)], [0]
+
+    def swapped(value, axis, bit):
+        count = lax.axis_size(axis)
+        return lax.ppermute(value, axis, [(i, i ^ bit) for i in range(count)])
+
+    half = rows // 2
+    by_one, by_two = swapped(own, "fsdp", 1), swapped(own, "fsdp", 2)
+    upper = swapped(by_two[:half], "fsdp", 1)
+    under = swapped(by_one[half:], "fsdp", 2)
+    mine = [own, by_one, by_two, upper, under]
+    place = lax.axis_index("fsdp")
+    core = lax.axis_index("ctx")
+    shards, starts = [], []
+    for other in (0, 1):
+        for value, bits, offset in zip(mine, (0, 1, 2, 3, 3), (0, 0, 0, 0, half)):
+            shards.append(swapped(value, "ctx", 1) if other else value)
+            starts.append(((place ^ bits) * 2 + (core ^ other)) * rows + offset)
+    return shards, starts
 
 
 def token_marks(segment, before):
@@ -653,10 +866,10 @@
         ],
         1,
     )
-    w_in = lax.all_gather(packed, shards, axis=0, tiled=True)
+    w_shards, w_starts = gathered_shards(packed)
+    w_starts = jnp.stack([jnp.asarray(start, jnp.int32) for start in w_starts])
     wo = lax.all_gather(w_out.T, shards, axis=0, tiled=True)
     gain_at = 2 * inner + 2 * state_size + 4 * heads
-    gain = w_in[:, gain_at].astype(F32)[None, :]
 
     edge, edge_segment = passed_along((hid[rows - EDGE :], segment[rows - 3 :]), "ctx", 1)
     tok = token_marks(segment, edge_segment)
@@ -682,41 +895,110 @@
         [jnp.repeat(skip_d, head_size)[None], out_gain[None], jnp.zeros((6, inner), F32)], 0
     )
 
-    normed, gate, pre, u, rec, st, pdx, state_end, decay_end = front(
-        hid, edge, tok, w_in, gain, conv_rows, dtp, inner, wide
+    normed, gate, pre, u, rec, st, pdx, state_end, decay_end, w_in, gain = front(
+        hid, edge, tok, w_shards, w_starts, 4 * heads, conv_rows, dtp, inner, wide
     )
     sin = chained(state_end, decay_end[:1], "ctx", 1)
-    scan, dgate, sums, part = middle(u, rec, gate, st, pdx, sin, cot, wo, prm)
-    sums = lax.psum(sums, "tp")
-    out_sum = lax.psum(part, "tp")
     inner_total = inner * lax.axis_size("tp")
-    dscan, dgr, glow, adj, psx, adj_start, out_gain_acc = turn(
-        scan, gate, dgate, sums, u, rec, prm, inner_total
-    )
+    halves_out = [None, None]
+    parts = [None] * GROUPS
+    for half in (1, 0):
+        scan, dgate, sums, parts[2 * half], parts[2 * half + 1] = middle(
+            u, rec, gate, st, pdx, sin, cot, wo, prm, half
+        )
+        halves_out[half] = (scan, dgate, butterfly_sum(sums, "tp"))
+    me = lax.axis_index("tp")
+    outer = jnp.full((8, LANES), (me == 0) | (me == lax.axis_size("tp") - 1), F32)
+    out_sums = [LineSum(parts[group], "tp") for group in range(GROUPS)]
+    turned = [None, None]
+    adj_start, decay_start = jnp.zeros_like(state_end), jnp.ones_like(decay_end)
+    out_gain_acc = 0.0
+    for half in (1, 0):
+        scan, dgate, sums = halves_out[half]
+        *turned[half], adj_start, gain_part, decay_start = turn(
+            scan, gate, dgate, sums, u, rec, prm, adj_start, decay_start, inner_total, half
+        )
+        out_gain_acc = out_gain_acc + gain_part
     ain = chained(adj_start, decay_end[:1], "ctx", -1)
-    inv_gate = lax.rsqrt(sums[0] / inner_total + EPSILON)[:, None]
-    block_out = (hid.astype(F32) + inv_gate * out_sum.astype(F32)).astype(BF16)
-
-    backs = []
-    for group in range(GROUPS):
-        backs.append(back(u, rec, dscan, st, pdx, sin, adj, psx, ain, prm, dtp, group))
+
     group_rows = rows // GROUPS
-    heads_of = [
-        jnp.concatenate([backs[g][0][:8], rec[g * group_rows : g * group_rows + 8]], 1)
-        for g in range(GROUPS)
-    ]
-    follows = heads_of[1:] + [passed_along(heads_of[0], "ctx", -1)]
-    rears = []
-    d_normed = []
-    for group in range(GROUPS):
-        rears.append(
-            rear(
-                backs[group][0], rec, pre, dgr, backs[group][1], follows[group], hid, w_in,
-                conv_rows, group,
-            )
+    backs = [None] * GROUPS
+    rears = [None] * GROUPS
+    d_normed = [None] * GROUPS
+    follows = [None] * GROUPS
+    dproj = rec[:8]
+
+    def run_back(group, after):
+        dscan, _, _, adj, psx = turned[group // (GROUPS // 2)]
+        backs[group] = back(u, rec, dscan, st, pdx, sin, adj, psx, ain, prm, dtp, after, group)
+        start = jnp.concatenate(
+            [backs[group][0][:8], rec[group * group_rows : group * group_rows + 8]], 1
         )
-        d_normed.append(lax.psum(rears[-1][1], "tp"))
-    dproj = jnp.concatenate([r[0] for r in rears], 0)
+        if group == 0:
+            follows[GROUPS - 1] = passed_along(start, "ctx", -1)
+        else:
+            follows[group - 1] = start
+
+    def run_rear(group, filled, after):
+        dgr = turned[group // (GROUPS // 2)][1]
+        rears[group] = rear(
+            backs[group][0], rec, pre, dgr, backs[group][1], follows[group], hid, w_in,
+            conv_rows, filled, after, group,
+        )
+        d_normed[group] = LineSum(rears[group][1], "tp")
+        return rears[group][0]
+
+    def settle(group, filled, after=()):
+        total = out_sums[group]
+        return by_group(
+            functools.partial(settle_kernel, float(inner_total)), hid, BF16, group, filled is None,
+            [
+                (hid, "all"),
+                (halves_out[group // (GROUPS // 2)][2], "half"),
+                (total.given, "group"),
+                (total.across, "group"),
+                (outer, "whole"),
+            ],
+            outer if filled is None else filled, after, "settle",
+        )
+
+    def finish(group, filled, after):
+        total = d_normed[group]
+        return by_group(
+            finish_kernel, hid, F32, group, filled is None,
+            [
+                (hid, "all"),
+                (cot, "all"),
+                (gain, "whole"),
+                (total.given, "group"),
+                (total.across, "group"),
+                (outer, "whole"),
+            ],
+            outer if filled is None else filled, after, "finish",
+        )
+
+    sum_a, sum_b, sum_c, sum_d = (out_sums[group] for group in (2, 3, 0, 1))
+    sum_a.inwards((decay_start,))
+    run_back(0, (sum_a.near,))
+    run_back(1, (backs[0][3],))
+    sum_b.inwards((backs[1][3],))
+    sum_a.middle((backs[1][3],))
+    dproj = run_rear(0, dproj, (sum_b.near, sum_a.across))
+    run_back(2, (rears[0][3],))
+    sum_c.inwards((backs[2][3],))
+    sum_b.middle((backs[2][3],))
+    dproj = run_rear(1, dproj, (sum_c.near, sum_b.across))
+    run_back(3, (rears[1][3],))
+    sum_d.inwards((backs[3][3],))
+    sum_c.middle((backs[3][3],))
+    block_out = settle(2, None, (backs[3][3],))
+    dproj = run_rear(2, dproj, (sum_d.near, sum_c.across, block_out))
+    dproj = run_rear(3, dproj, (rears[2][3],))
+    d_normed[0].inwards((rears[3][3],))
+    sum_d.middle((rears[3][3],))
+    block_out = settle(3, block_out, (rears[3][3],))
+
+    glow = jnp.concatenate([turned[0][2], turned[1][2]], 0)
     conv_acc = sum(r[2] for r in rears)
     gain_acc = sum(r[3][0] for r in rears)
     skip_acc = sum(b[2][0] for b in backs)
@@ -725,6 +1007,10 @@
     contract_rows = (((0,), (0,)), ((), ()))
     w_grad = lax.dot_general(normed, dproj, contract_rows, preferred_element_type=F32)
     wo_grad = lax.dot_general(cot, glow, contract_rows, preferred_element_type=F32)
+    for group in range(GROUPS):
+        if group:
+            d_normed[group].inwards((w_grad[:8, :LANES],))
+        d_normed[group].middle((w_grad[:8, :LANES],))
     w_grad = w_grad.at[:, gain_at].set(gain_acc)
     w_owned = lax.psum_scatter(w_grad, shards, scatter_dimension=0, tiled=True)
     wo_owned = lax.psum_scatter(wo_grad, shards, scatter_dimension=0, tiled=True)
@@ -737,7 +1023,7 @@
             head_acc[:2].reshape(-1),
         ]
     )
-    small = lax.psum(small, shards)
+    small = butterfly_sum(butterfly_sum(small, "ctx"), "fsdp")
     conv_sum = small[: (taps + 1) * wide].reshape(taps + 1, wide)
     rest = small[(taps + 1) * wide :]
     shared = jnp.concatenate(
@@ -747,24 +1033,17 @@
             conv_sum[:, inner:].reshape(-1),
         ]
     )
-    shared = lax.psum(shared, "tp")
+    shared = butterfly_sum(shared, "tp")
     bc_size = owned * 2 * state_size
     bc_owned = shared[:bc_size].reshape(owned, 2, state_size)
     gain_owned = shared[bc_size : bc_size + owned]
     conv_bc = shared[bc_size + owned :].reshape(taps + 1, 2, state_size)
 
-    tokens = hid.astype(F32)
-    inv_rms = lax.rsqrt(jnp.mean(tokens * tokens, -1, keepdims=True) + EPSILON)
-    grads = []
+    block_out = settle(0, block_out)
+    block_out = settle(1, block_out)
+    hidden_grad = None
     for group in range(GROUPS):
-        span = slice(group * group_rows, (group + 1) * group_rows)
-        scaled = d_normed[group].astype(F32) * gain
-        inv = inv_rms[span]
-        cross = jnp.sum(scaled * tokens[span], -1, keepdims=True) / width
-        grads.append(
-            cot[span].astype(F32) + inv * scaled - tokens[span] * (inv * inv * inv * cross)
-        )
-    hidden_grad = jnp.concatenate(grads, 0)
+        hidden_grad = finish(group, hidden_grad, (block_out,))
 
     return (
         block_out[None],

time: 700 us -> 572 us (0.82)
  waiting for transfers between devices: 420 us -> 150 us
  starting transfers between devices: 9.15 us -> 103 us
  Pallas kernels: 132 us -> 207 us
  blocking collectives: 26 us -> 0 us
  other arithmetic: 33.9 us -> 16.3 us
  local copies, waits for them, and re-layouts: 37.9 us -> 52.6 us
    psum x3 -> x0, waiting for transfers between devices: 331 us -> none  [the longest x1 284 us: body(): out_sum = lax.psum(part, 'tp')]
    ppermute x0 -> x42, waiting for transfers between devices: none -> 147 us  [the longest x8 68.8 us: middle(): self.given = lax.ppermute(self.across, self.axis, [(1, 0), (2, 3)])]
    ppermute x0 -> x42, starting transfers between devices: none -> 94.6 us  [the longest x8 34.1 us: __init__(): self.come = lax.ppermute(value, axis, [(0, 1), (3, 2)])]
    pallas_call x10 -> x35, Pallas kernels: 118 us -> 190 us  [the longest x4 47.2 us: back(): pl.pallas_call(ordered(back_kernel, 11, len(after)), grid=(steps,), in_sp...]
    reduce_scatter x1, waiting for transfers between devices: 40.2 us -> 0.01 us  [body(): lax.psum_scatter(wo_grad, shards, scatter_dimension=0, tiled=True)]
    psum x1 -> x0, blocking collectives: 26 us -> none  [body(): small = lax.psum(small, shards)]
    reduce_scatter x1, waiting for transfers between devices: 24.2 us -> 0.01 us  [body(): w_owned = lax.psum_scatter(w_grad, shards, scatter_dimension=0, tiled=True)]
    all_gather x1 -> x0, waiting for transfers between devices: 22.6 us -> none  [body(): w_in = lax.all_gather(packed, shards, axis=0, tiled=True)]
  transfers between devices with their start and end apart: 12 -> 50, of which waited for: 8 -> 13; matrix products, arithmetic and copies ran while one was open for 9% -> 9% of each run, Pallas kernels for 12% -> 34%
where the time goes in v2:
time: 572 us; the launch traced here: 561 us
  Pallas kernels  207 us (36%)
  waiting for transfers between devices  150 us (26%)
  starting transfers between devices  103 us (18%)
  local copies, waits for them, and re-layouts  52.6 us (9%)
  matrix products  17 us (3%)
  other arithmetic  16.3 us (3%)
  between operations  15.1 us (3%)
    ppermute x8, waiting for transfers between devices, middle(): self.given = lax.ppermute(self.across, self.axis, [(1, 0), (2, 3)])  68.8 us
    pallas_call x4, Pallas kernels, back(): pl.pallas_call(ordered(back_kernel, 11, len(after)), grid=(steps,), in_sp...  47.2 us
    ppermute x8, waiting for transfers between devices, __init__(): self.come = lax.ppermute(value, axis, [(0, 1), (3, 2)])  41.1 us
    pallas_call x16, Pallas kernels, join(): pl.pallas_call(ordered(join_kernel, 2, len(after)), grid=(rows // STEP,),...  39.3 us
    ppermute x8, starting transfers between devices, __init__(): self.come = lax.ppermute(value, axis, [(0, 1), (3, 2)])  34.1 us
    ppermute x9, waiting for transfers between devices, butterfly_sum(): value = value + lax.ppermute(value, axis, pairs)  33.4 us
    ppermute x9, starting transfers between devices, butterfly_sum(): value = value + lax.ppermute(value, axis, pairs)  32.7 us
    pallas_call x4, Pallas kernels, rear(): pl.pallas_call(ordered(rear_kernel, 10, len(after)), grid=(steps,), in_sp...  29.7 us
  transfers between devices with their start and end apart: 50, of which 13 were waited for; matrix products, arithmetic and copies ran while one was open for 9% of the time, Pallas kernels for 34%

profile of v2, /device:TPU:0, one launch (start us, length us, event | category | flops | bytes accessed | tf_op | source)
XLA Modules:
  0.0 560.8 jit_solution(8509377815277379423)
XLA Ops:
  11.3 2.6 collective-permute-start.3
  33.7 3.6 collective-permute-done.4.refs_3_
  41.5 25.6 %front.1 = (bf16[2048,1024]{1,0:T(8,128)(2,1)}, f32[2048,512]{1,0:T(8,128)}, f32[2048,768]{1,0:T(8,128)}, f32[2048,768]{1,0:T(8,128)}, f32[2048,128]{1,0:T(8,128...) custom-call(s32[10]{0:T(128)} %stack.67.starts, ...), custom_call_target="tpu_custom_call" | custom-call | bytes 3690000 | tf_op jit(solution)/shard_map/front/pallas_call | solution.py:170
  71.5 10.7 %middle.3 = (f32[1024,512]{1,0:T(8,128)}, f32[1024,512]{1,0:T(8,128)}, f32[8,1024]{1,0:T(8,128)}, bf16[512,1024]{1,0:T(8,128)(2,1)}, bf16[512,1024]{1,0:T(8,128)(2,1)}) custom-call(f32[2048,768]{1,0:T(8,128)} %get-tuple-element.95.u.upre_c.refs_0_, f32[2048,128]{1,0:T(8,128)} %get-tuple-element.96.rec.refs_1_, f32[2048,512]{1,0:T(8,128)} %get-tuple-element.97.gate, ...), custom_call_target="tpu_custom_call" | custom-call | bytes 3690000 | tf_op jit(solution)/shard_map/middle/pallas_call | solution.py:293
  82.2 3.5 collective-permute-start.18
  87.2 10.7 %middle.2 = (f32[1024,512]{1,0:T(8,128)}, f32[1024,512]{1,0:T(8,128)}, f32[8,1024]{1,0:T(8,128)}, bf16[512,1024]{1,0:T(8,128)(2,1)}, bf16[512,1024]{1,0:T(8,128)(2,1)}) custom-call(f32[2048,768]{1,0:T(8,128)} %get-tuple-element.95.u.upre_c.refs_0_, f32[2048,128]{1,0:T(8,128)} %get-tuple-element.96.rec.refs_1_, f32[2048,512]{1,0:T(8,128)} %get-tuple-element.97.gate, ...), custom_call_target="tpu_custom_call" | custom-call | bytes 3690000 | tf_op jit(solution)/shard_map/middle/pallas_call | solution.py:293
  99.9 32.5 %collective-permute-done.15 = f32[8,1024]{1,0:T(8,128)S(1)} collective-permute-done((f32[8,1024]{1,0:T(8,128)}, f32[8,1024]{1,0:T(8,128)S(1)}, u32[]{:S(2)}, u32[]{:S(2)}) %collective-permute-start.15) | collective-permute-done | bytes 32800 | tf_op jit(solution)/shard_map/ppermute | solution.py:758
  132.4 3.5 collective-permute-start.16
  139.8 8.1 %turn.2 = (f32[1024,512]{1,0:T(8,128)}, bf16[1024,512]{1,0:T(8,128)(2,1)}, bf16[1024,512]{1,0:T(8,128)(2,1)}, f32[8,128,512]{2,1,0:T(8,128)}, f32[64,512]{1,0:T(...) custom-call(f32[1024,512]{1,0:T(8,128)} %get-tuple-element.103.scan, ...), custom_call_target="tpu_custom_call" | custom-call | bytes 3690000 | tf_op jit(solution)/shard_map/turn/pallas_call | solution.py:394
  148.5 8.2 %turn.3 = (f32[1024,512]{1,0:T(8,128)}, bf16[1024,512]{1,0:T(8,128)(2,1)}, bf16[1024,512]{1,0:T(8,128)(2,1)}, f32[8,128,512]{2,1,0:T(8,128)}, f32[64,512]{1,0:T(...) custom-call(f32[1024,512]{1,0:T(8,128)} %get-tuple-element.109.scan, ...), custom_call_target="tpu_custom_call" | custom-call | bytes 3690000 | tf_op jit(solution)/shard_map/turn/pallas_call | solution.py:394
  157.6 2.5 join.16.refs_11_.refs_0_
  160.8 6.6 %collective-permute-start.21 = (bf16[512,1024]{1,0:T(8,128)(2,1)S(1)}, bf16[512,1024]{1,0:T(8,128)(2,1)S(1)}, u32[]{:S(2)}, u32[]{:S(2)}) collective-permute-start(bf16[512,1024]{1,0:T(8,128)(2,1)S(1)} %copy-done.15), channel_id=1, source_target_pairs={{0,1},{3,2},{4,5},{7,6},{8,9},{11,10},{12,13},{15,14},{16,17},{19,... | collective-permute-start | bytes 3145736 | tf_op jit(solution)/shard_map/ppermute | solution.py:792
  171.8 11.8 %back.4 = (f32[512,768]{1,0:T(8,128)}, bf16[512,128]{1,0:T(8,128)(2,1)}, f32[8,512]{1,0:T(8,128)}, f32[8,128]{1,0:T(8,128)}) custom-call(f32[2048,768]{1,0:T(8,128)} %get-tuple-element.95.u.upre_c.refs_0_, f32[2048,128]{1,0:T(8,128)} %get-tuple-element.96.rec.refs_1_, f32[1024,512]{1,0:T(8,128)} %get-tuple-element.114.refs_2_, ...), custom_call_target="tpu_custom_call" | custom-call | bytes 3690000 | tf_op jit(solution)/shard_map/back/pallas_call | solution.py:561
  183.6 11.9 %back.5 = (f32[512,768]{1,0:T(8,128)}, bf16[512,128]{1,0:T(8,128)(2,1)}, f32[8,512]{1,0:T(8,128)}, f32[8,128]{1,0:T(8,128)}) custom-call(f32[2048,768]{1,0:T(8,128)} %get-tuple-element.95.u.upre_c.refs_0_, f32[2048,128]{1,0:T(8,128)} %get-tuple-element.96.rec.refs_1_, f32[1024,512]{1,0:T(8,128)} %get-tuple-element.114.refs_2_, ...), custom_call_target="tpu_custom_call" | custom-call | bytes 3690000 | tf_op jit(solution)/shard_map/back/pallas_call | solution.py:561
  206.1 2.5 join.18.refs_11_.refs_3_
  208.5 7.4 %rear.4 = (bf16[2048,1408]{1,0:T(8,128)(2,1)}, bf16[512,1024]{1,0:T(8,128)(2,1)}, f32[8,768]{1,0:T(8,128)}, f32[8,1024]{1,0:T(8,128)}) custom-call(f32[512,768]{1,0:T(8,128)} %get-tuple-element.124.refs_0_, f32[2048,128]{1,0:T(8,128)} %get-tuple-element.96.rec.refs_1_, f32[2048,768]{1,0:T(8,128)} %get-tuple-element.121.refs_2_, ...), custom_call_target="tpu_custom_call" | custom-call | bytes 3690000 | tf_op jit(solution)/shard_map/rear/pallas_call | solution.py:656
  216.0 11.8 %back.6 = (f32[512,768]{1,0:T(8,128)}, bf16[512,128]{1,0:T(8,128)(2,1)}, f32[8,512]{1,0:T(8,128)}, f32[8,128]{1,0:T(8,128)}) custom-call(f32[2048,768]{1,0:T(8,128)} %get-tuple-element.95.u.upre_c.refs_0_, f32[2048,128]{1,0:T(8,128)} %get-tuple-element.96.rec.refs_1_, f32[1024,512]{1,0:T(8,128)} %get-tuple-element.106.refs_2_, ...), custom_call_target="tpu_custom_call" | custom-call | bytes 3690000 | tf_op jit(solution)/shard_map/back/pallas_call | solution.py:561
  240.9 7.4 %rear.5 = (bf16[2048,1408]{1,0:T(8,128)(2,1)}, bf16[512,1024]{1,0:T(8,128)(2,1)}, f32[8,768]{1,0:T(8,128)}, f32[8,1024]{1,0:T(8,128)}) custom-call(f32[512,768]{1,0:T(8,128)} %get-tuple-element.120.refs_0_, f32[2048,128]{1,0:T(8,128)} %get-tuple-element.96.rec.refs_1_, f32[2048,768]{1,0:T(8,128)} %get-tuple-element.121.refs_2_, ...), custom_call_target="tpu_custom_call", output_to_operand_aliasing={{0}: (9, {})} | custom-call | bytes 3690000 | tf_op jit(solution)/shard_map/rear/pallas_call | solution.py:656
  248.3 11.8 %back.7 = (f32[512,768]{1,0:T(8,128)}, bf16[512,128]{1,0:T(8,128)(2,1)}, f32[8,512]{1,0:T(8,128)}, f32[8,128]{1,0:T(8,128)}) custom-call(f32[2048,768]{1,0:T(8,128)} %get-tuple-element.95.u.upre_c.refs_0_, f32[2048,128]{1,0:T(8,128)} %get-tuple-element.96.rec.refs_1_, f32[1024,512]{1,0:T(8,128)} %get-tuple-element.106.refs_2_, ...), custom_call_target="tpu_custom_call" | custom-call | bytes 3690000 | tf_op jit(solution)/shard_map/back/pallas_call | solution.py:561
  264.9 2.5 join.22.refs_11_.refs_3_
  267.9 3.0 settle.4.refs_12_.refs_5_
  271.0 7.4 %rear.6 = (bf16[2048,1408]{1,0:T(8,128)(2,1)}, bf16[512,1024]{1,0:T(8,128)(2,1)}, f32[8,768]{1,0:T(8,128)}, f32[8,1024]{1,0:T(8,128)}) custom-call(f32[512,768]{1,0:T(8,128)} %get-tuple-element.130.refs_0_, f32[2048,128]{1,0:T(8,128)} %get-tuple-element.96.rec.refs_1_, f32[2048,768]{1,0:T(8,128)} %get-tuple-element.121.refs_2_, ...), custom_call_target="tpu_custom_call", output_to_operand_aliasing={{0}: (9, {})} | custom-call | bytes 3690000 | tf_op jit(solution)/shard_map/rear/pallas_call | solution.py:656
  279.0 7.4 %rear.7 = (bf16[2048,1408]{1,0:T(8,128)(2,1)}, bf16[512,1024]{1,0:T(8,128)(2,1)}, f32[8,768]{1,0:T(8,128)}, f32[8,1024]{1,0:T(8,128)}) custom-call(f32[512,768]{1,0:T(8,128)} %get-tuple-element.136.refs_0_, f32[2048,128]{1,0:T(8,128)} %get-tuple-element.96.rec.refs_1_, f32[2048,768]{1,0:T(8,128)} %get-tuple-element.121.refs_2_, ...), custom_call_target="tpu_custom_call", output_to_operand_aliasing={{0}: (9, {})} | custom-call | bytes 3690000 | tf_op jit(solution)/shard_map/rear/pallas_call | solution.py:656
  287.5 10.5 %fusion.20 = f32[1024,1408]{1,0:T(8,128)S(1)} fusion(bf16[2048,1024]{1,0:T(8,128)(2,1)} %get-tuple-element.146, bf16[2048,1408]{1,0:T(8,128)(2,1)} %get-tuple-element.147), kind=kOutput, calls=%fused_computation.55 | convolution fusion | flops 5905580032 | bytes 15728640 | tf_op jit(solution)/shard_map/dot_general | solution.py:1008
  298.0 2.6 copy.108
  306.9 6.5 %collective-permute-start.39 = (bf16[512,1024]{1,0:T(8,128)(2,1)S(1)}, bf16[512,1024]{1,0:T(8,128)(2,1)}, u32[]{:S(2)}, u32[]{:S(2)}) collective-permute-start(bf16[512,1024]{1,0:T(8,128)(2,1)S(1)} %copy-done.9), channel_id=1, source_target_pairs={{0,1},{3,2},{4,5},{7,6},{8,9},{11,10},{12,13},{15,14},{16,17},{19,... | collective-permute-start | bytes 3145736 | tf_op jit(solution)/shard_map/ppermute | solution.py:792
  315.4 6.5 %collective-permute-start.36 = (bf16[512,1024]{1,0:T(8,128)(2,1)}, bf16[512,1024]{1,0:T(8,128)(2,1)}, u32[]{:S(2)}, u32[]{:S(2)}) collective-permute-start(bf16[512,1024]{1,0:T(8,128)(2,1)} %get-tuple-element.149.refs_0_), channel_id=1, source_target_pairs={{0,1},{3,2},{4,5},{7,6},{8,9},{11,10},{12,13},{15,14},{16,17},{19,... | collective-permute-start | bytes 3145736 | tf_op jit(solution)/shard_map/ppermute | solution.py:792
  324.8 11.0 %collective-permute-done.39.refs_1_ = bf16[512,1024]{1,0:T(8,128)(2,1)} collective-permute-done((bf16[512,1024]{1,0:T(8,128)(2,1)S(1)}, bf16[512,1024]{1,0:T(8,128)(2,1)}, u32[]{:S(2)}, u32[]{:S(2)}) %collective-permute-start.39) | collective-permute-done | bytes 1048608 | tf_op jit(solution)/shard_map/ppermute | solution.py:792
  335.8 5.5 collective-permute-start.30
  343.5 6.5 %fusion.4 = f32[1024,512]{0,1:T(8,128)} fusion(bf16[1024,512]{1,0:T(8,128)(2,1)} %get-tuple-element.162, bf16[1024,512]{1,0:T(8,128)(2,1)} %get-tuple-element.161, bf16[1,2048,1024]{2,1,0:T(8,128)(2,1)} %param.20), kind=kOutput, calls=%fused_computation.4 | convolution fusion | flops 2151677952 | bytes 8388608 | tf_op jit(solution)/shard_map/dot_general | solution.py:1009
  350.0 8.3 %collective-permute-done.36.refs_1_ = bf16[512,1024]{1,0:T(8,128)(2,1)} collective-permute-done((bf16[512,1024]{1,0:T(8,128)(2,1)}, bf16[512,1024]{1,0:T(8,128)(2,1)}, u32[]{:S(2)}, u32[]{:S(2)}) %collective-permute-start.36) | collective-permute-done | bytes 1048608 | tf_op jit(solution)/shard_map/ppermute | solution.py:792
  365.9 3.1 settle.5.refs_5_
  377.1 3.7 collective-permute-done.30.refs_1_
  380.8 2.5 join.24.refs_0_
  385.1 18.2 %collective-permute-done.33.refs_1_ = bf16[512,1024]{1,0:T(8,128)(2,1)} collective-permute-done((bf16[512,1024]{1,0:T(8,128)(2,1)}, bf16[512,1024]{1,0:T(8,128)(2,1)}, u32[]{:S(2)}, u32[]{:S(2)}) %collective-permute-start.33) | collective-permute-done | bytes 1048608 | tf_op jit(solution)/shard_map/ppermute | solution.py:792
  409.9 4.4 collective-permute-start.45
  418.3 2.5 join.29.refs_4_
  425.9 2.5 join.25.refs_4_
  434.7 14.1 %collective-permute-done.27.refs_2_ = bf16[512,1024]{1,0:T(8,128)(2,1)S(1)} collective-permute-done((bf16[512,1024]{1,0:T(8,128)(2,1)S(1)}, bf16[512,1024]{1,0:T(8,128)(2,1)S(1)}, u32[]{:S(2)}, u32[]{:S(2)}) %collective-permute-start.27) | collective-permute-done | bytes 1048608 | tf_op jit(solution)/shard_map/ppermute | solution.py:802
  448.8 19.8 %collective-permute-start.46 = (f32[34176]{0:T(1024)S(1)}, f32[34176]{0:T(1024)S(1)}, u32[]{:S(2)}, u32[]{:S(2)}) collective-permute-start(f32[34176]{0:T(1024)S(1)} %fusion.23), channel_id=1, source_target_pairs={{0,2},{1,3},{2,0},{3,1},{4,6},{5,7},{6,4},{7,5},{8,10},{9,11},{10,... | collective-permute-start | bytes 410120 | tf_op jit(solution)/shard_map/ppermute | solution.py:758
  469.9 3.3 settle.6.refs_5_
  473.2 3.1 settle.7.refs_7_
  476.2 20.5 %collective-permute-done.41.refs_3_ = bf16[512,1024]{1,0:T(8,128)(2,1)S(1)} collective-permute-done((bf16[512,1024]{1,0:T(8,128)(2,1)}, bf16[512,1024]{1,0:T(8,128)(2,1)S(1)}, u32[]{:S(2)}, u32[]{:S(2)}) %collective-permute-start.41) | collective-permute-done | bytes 1048608 | tf_op jit(solution)/shard_map/ppermute | solution.py:802
  497.7 3.7 finish.4.refs_6_
  502.3 3.7 finish.5.refs_6_
  506.0 34.2 %collective-permute-done.35.refs_3_ = bf16[512,1024]{1,0:T(8,128)(2,1)S(1)} collective-permute-done((bf16[512,1024]{1,0:T(8,128)(2,1)}, bf16[512,1024]{1,0:T(8,128)(2,1)S(1)}, u32[]{:S(2)}, u32[]{:S(2)}) %collective-permute-start.35) | collective-permute-done | bytes 1048608 | tf_op jit(solution)/shard_map/ppermute | solution.py:802
  541.2 3.7 finish.6.refs_6_
  545.9 3.7 finish.7
  (291 shorter events, 139.0 us)
Async XLA Ops:
  7.2 63.6 %all-gather.2.cloned.1.call-start = ((), (), s32[]{:S(2)}) async-start(), calls=%async_computation.2 | async-start | bytes 1179648 | tf_op jit(solution)/shard_map/all_gather | solution.py:871
  10.8 29.7 %collective-permute-start.6 = (bf16[128,1408]{1,0:T(8,128)(2,1)S(1)}, bf16[128,1408]{1,0:T(8,128)(2,1)S(1)}, u32[]{:S(2)}, u32[]{:S(2)}) collective-permute-start(bf16[128,1408]{1,0:T(8,128)(2,1)S(1)} %concatenate.61.refs_0_), channel_id=1, source_target_pairs={{0,4},{4,0},{1,5},{5,1},{2,6},{6,2},{3,7},{7,3},{8,12},{12,8},{9,1... | collective-permute-start | bytes 1081352 | tf_op jit(solution)/shard_map/ppermute | solution.py:812
  11.3 20.0 %collective-permute-start.3 = (bf16[128,1408]{1,0:T(8,128)(2,1)S(1)}, bf16[128,1408]{1,0:T(8,128)(2,1)S(1)}, u32[]{:S(2)}, u32[]{:S(2)}) collective-permute-start(bf16[128,1408]{1,0:T(8,128)(2,1)S(1)} %concatenate.61.refs_0_), channel_id=1, source_target_pairs={{0,16},{8,24},{16,0},{24,8},{1,17},{9,25},{17,1},{25,9},{2,18},{10... | collective-permute-start | bytes 1081352 | tf_op jit(solution)/shard_map/ppermute | solution.py:812
  13.9 18.0 %collective-permute-start.2 = (bf16[128,1408]{1,0:T(8,128)(2,1)S(1)}, bf16[128,1408]{1,0:T(8,128)(2,1)S(1)}, u32[]{:S(2)}, u32[]{:S(2)}) collective-permute-start(bf16[128,1408]{1,0:T(8,128)(2,1)S(1)} %concatenate.61.refs_0_), channel_id=1, source_target_pairs={{0,8},{8,0},{16,24},{24,16},{1,9},{9,1},{17,25},{25,17},{2,10},{10... | collective-permute-start | bytes 1081352 | tf_op jit(solution)/shard_map/ppermute | solution.py:812
  16.2 13.9 %collective-permute-start.1 = (s32[3]{0:T(128)S(1)}, s32[3]{0:T(128)S(1)}, u32[]{:S(2)}, u32[]{:S(2)}) collective-permute-start(s32[3]{0:T(128)S(1)} %slice_bitcast_fusion.4), channel_id=1, source_target_pairs={{0,4},{1,5},{2,6},{3,7},{8,12},{9,13},{10,14},{11,15},{16,20},{17,... | collective-permute-start | bytes 44 | tf_op jit(solution)/shard_map/ppermute | solution.py:743
  18.7 13.6 %collective-permute-start = (bf16[16,1024]{1,0:T(8,128)(2,1)S(1)}, bf16[16,1024]{1,0:T(8,128)(2,1)S(1)}, u32[]{:S(2)}, u32[]{:S(2)}) collective-permute-start(bf16[16,1024]{1,0:T(8,128)(2,1)S(1)} %slice_bitcast_fusion.1), channel_id=1, source_target_pairs={{0,4},{1,5},{2,6},{3,7},{8,12},{9,13},{10,14},{11,15},{16,20},{17,... | collective-permute-start | bytes 98312 | tf_op jit(solution)/shard_map/ppermute | solution.py:743
  21.7 385.7 %reduce-scatter.3.cloned.1.call-start = ((), (), s32[]{:S(2)}) async-start(), calls=%async_computation.3 | async-start | bytes 6488064 | tf_op jit(solution)/shard_map/reduce_scatter | solution.py:1015
  31.4 5.9 %collective-permute-start.4 = (bf16[64,1408]{1,0:T(8,128)(2,1)S(1)}, bf16[64,1408]{1,0:T(8,128)(2,1)S(1)}, u32[]{:S(2)}, u32[]{:S(2)}) collective-permute-start(bf16[64,1408]{1,0:T(8,128)(2,1)S(1)} %slice.262), channel_id=1, source_target_pairs={{0,8},{8,0},{16,24},{24,16},{1,9},{9,1},{17,25},{25,17},{2,10},{10... | collective-permute-start | bytes 540680 | tf_op jit(solution)/shard_map/ppermute | solution.py:812
  32.0 5.7 %collective-permute-start.5 = (bf16[64,1408]{1,0:T(8,128)(2,1)S(1)}, bf16[64,1408]{1,0:T(8,128)(2,1)}, u32[]{:S(2)}, u32[]{:S(2)}) collective-permute-start(bf16[64,1408]{1,0:T(8,128)(2,1)S(1)} %slice.263), channel_id=1, source_target_pairs={{0,16},{8,24},{16,0},{24,8},{1,17},{9,25},{17,1},{25,9},{2,18},{10... | collective-permute-start | bytes 540680 | tf_op jit(solution)/shard_map/ppermute | solution.py:812
  32.3 8.2 %collective-permute-start.8 = (bf16[128,1408]{1,0:T(8,128)(2,1)S(1)}, bf16[128,1408]{1,0:T(8,128)(2,1)S(1)}, u32[]{:S(2)}, u32[]{:S(2)}) collective-permute-start(bf16[128,1408]{1,0:T(8,128)(2,1)S(1)} %collective-permute-done.3.refs_2_), channel_id=1, source_target_pairs={{0,4},{4,0},{1,5},{5,1},{2,6},{6,2},{3,7},{7,3},{8,12},{12,8},{9,1... | collective-permute-start | bytes 1081352 | tf_op jit(solution)/shard_map/ppermute | solution.py:812
  32.3 8.2 %collective-permute-start.7 = (bf16[128,1408]{1,0:T(8,128)(2,1)S(1)}, bf16[128,1408]{1,0:T(8,128)(2,1)S(1)}, u32[]{:S(2)}, u32[]{:S(2)}) collective-permute-start(bf16[128,1408]{1,0:T(8,128)(2,1)S(1)} %collective-permute-done.2.refs_1_), channel_id=1, source_target_pairs={{0,4},{4,0},{1,5},{5,1},{2,6},{6,2},{3,7},{7,3},{8,12},{12,8},{9,1... | collective-permute-start | bytes 1081352 | tf_op jit(solution)/shard_map/ppermute | solution.py:812
  67.1 3.7 collective-permute-start.11
  82.2 74.5 %collective-permute-start.18 = (bf16[512,1024]{1,0:T(8,128)(2,1)}, bf16[512,1024]{1,0:T(8,128)(2,1)S(1)}, u32[]{:S(2)}, u32[]{:S(2)}) collective-permute-start(bf16[512,1024]{1,0:T(8,128)(2,1)} %get-tuple-element.117.refs_0_), channel_id=1, source_target_pairs={{0,1},{3,2},{4,5},{7,6},{8,9},{11,10},{12,13},{15,14},{16,17},{19,... | collective-permute-start | bytes 3145736 | tf_op jit(solution)/shard_map/ppermute | solution.py:792
  85.7 109.7 %collective-permute-start.19 = (bf16[512,1024]{1,0:T(8,128)(2,1)}, bf16[512,1024]{1,0:T(8,128)(2,1)S(1)}, u32[]{:S(2)}, u32[]{:S(2)}) collective-permute-start(bf16[512,1024]{1,0:T(8,128)(2,1)} %get-tuple-element.127.refs_0_), channel_id=1, source_target_pairs={{0,1},{3,2},{4,5},{7,6},{8,9},{11,10},{12,13},{15,14},{16,17},{19,... | collective-permute-start | bytes 3145736 | tf_op jit(solution)/shard_map/ppermute | solution.py:792
  87.1 45.3 %collective-permute-start.15 = (f32[8,1024]{1,0:T(8,128)}, f32[8,1024]{1,0:T(8,128)S(1)}, u32[]{:S(2)}, u32[]{:S(2)}) collective-permute-start(f32[8,1024]{1,0:T(8,128)} %get-tuple-element.105), channel_id=1, source_target_pairs={{0,1},{1,0},{2,3},{3,2},{4,5},{5,4},{6,7},{7,6},{8,9},{9,8},{10,11... | collective-permute-start | bytes 98312 | tf_op jit(solution)/shard_map/ppermute | solution.py:758
  97.8 38.1 %collective-permute-start.12 = (f32[8,1024]{1,0:T(8,128)}, f32[8,1024]{1,0:T(8,128)S(1)}, u32[]{:S(2)}, u32[]{:S(2)}) collective-permute-start(f32[8,1024]{1,0:T(8,128)} %get-tuple-element.101), channel_id=1, source_target_pairs={{0,1},{1,0},{2,3},{3,2},{4,5},{5,4},{6,7},{7,6},{8,9},{9,8},{10,11... | collective-permute-start | bytes 98312 | tf_op jit(solution)/shard_map/ppermute | solution.py:758
  132.4 5.4 collective-permute-start.16
  136.7 11.1 %collective-permute-start.13 = (f32[8,1024]{1,0:T(8,128)S(1)}, f32[8,1024]{1,0:T(8,128)S(1)}, u32[]{:S(2)}, u32[]{:S(2)}) collective-permute-start(f32[8,1024]{1,0:T(8,128)S(1)} %add.141), channel_id=1, source_target_pairs={{0,2},{1,3},{2,0},{3,1},{4,6},{5,7},{6,4},{7,5},{8,10},{9,11},{10,... | collective-permute-start | bytes 98312 | tf_op jit(solution)/shard_map/ppermute | solution.py:758
  160.1 45.0 %collective-permute-start.20 = (bf16[512,1024]{1,0:T(8,128)(2,1)}, bf16[512,1024]{1,0:T(8,128)(2,1)S(1)}, u32[]{:S(2)}, u32[]{:S(2)}) collective-permute-start(bf16[512,1024]{1,0:T(8,128)(2,1)} %join.16.refs_11_.refs_0_), channel_id=1, source_target_pairs={{1,2},{2,1},{5,6},{6,5},{9,10},{10,9},{13,14},{14,13},{17,18},{18,... | collective-permute-start | bytes 3145736 | tf_op jit(solution)/shard_map/ppermute | solution.py:797
  160.8 67.0 %collective-permute-start.21 = (bf16[512,1024]{1,0:T(8,128)(2,1)S(1)}, bf16[512,1024]{1,0:T(8,128)(2,1)S(1)}, u32[]{:S(2)}, u32[]{:S(2)}) collective-permute-start(bf16[512,1024]{1,0:T(8,128)(2,1)S(1)} %copy-done.15), channel_id=1, source_target_pairs={{0,1},{3,2},{4,5},{7,6},{8,9},{11,10},{12,13},{15,14},{16,17},{19,... | collective-permute-start | bytes 3145736 | tf_op jit(solution)/shard_map/ppermute | solution.py:792
  167.4 3.6 collective-permute-start.17
  198.8 39.0 %collective-permute-start.22 = (bf16[512,1024]{1,0:T(8,128)(2,1)}, bf16[512,1024]{1,0:T(8,128)(2,1)}, u32[]{:S(2)}, u32[]{:S(2)}) collective-permute-start(bf16[512,1024]{1,0:T(8,128)(2,1)} %join.17.refs_10_.refs_0_), channel_id=1, source_target_pairs={{1,2},{2,1},{5,6},{6,5},{9,10},{10,9},{13,14},{14,13},{17,18},{18,... | collective-permute-start | bytes 3145736 | tf_op jit(solution)/shard_map/ppermute | solution.py:797
  201.8 59.6 %collective-permute-start.14 = (bf16[512,1024]{1,0:T(8,128)(2,1)S(1)}, bf16[512,1024]{1,0:T(8,128)(2,1)S(1)}, u32[]{:S(2)}, u32[]{:S(2)}) collective-permute-start(bf16[512,1024]{1,0:T(8,128)(2,1)S(1)} %copy-done.14), channel_id=1, source_target_pairs={{0,1},{3,2},{4,5},{7,6},{8,9},{11,10},{12,13},{15,14},{16,17},{19,... | collective-permute-start | bytes 3145736 | tf_op jit(solution)/shard_map/ppermute | solution.py:792
  231.2 33.6 %collective-permute-start.25 = (bf16[512,1024]{1,0:T(8,128)(2,1)}, bf16[512,1024]{1,0:T(8,128)(2,1)}, u32[]{:S(2)}, u32[]{:S(2)}) collective-permute-start(bf16[512,1024]{1,0:T(8,128)(2,1)} %join.19.refs_10_.refs_0_), channel_id=1, source_target_pairs={{1,2},{2,1},{5,6},{6,5},{9,10},{10,9},{13,14},{14,13},{17,18},{18,... | collective-permute-start | bytes 3145736 | tf_op jit(solution)/shard_map/ppermute | solution.py:797
  232.9 34.4 %collective-permute-start.26 = (bf16[512,1024]{1,0:T(8,128)(2,1)S(1)}, bf16[512,1024]{1,0:T(8,128)(2,1)}, u32[]{:S(2)}, u32[]{:S(2)}) collective-permute-start(bf16[512,1024]{1,0:T(8,128)(2,1)S(1)} %copy-done.4), channel_id=1, source_target_pairs={{1,0},{2,3},{5,4},{6,7},{9,8},{10,11},{13,12},{14,15},{17,16},{18,... | collective-permute-start | bytes 3145736 | tf_op jit(solution)/shard_map/ppermute | solution.py:802
  235.6 42.8 %collective-permute-start.24 = (f32[8,896]{1,0:T(8,128)S(1)}, f32[8,896]{1,0:T(8,128)S(1)}, u32[]{:S(2)}, u32[]{:S(2)}) collective-permute-start(f32[8,896]{1,0:T(8,128)S(1)} %pad_maximum_fusion.3), channel_id=1, source_target_pairs={{4,0},{5,1},{6,2},{7,3},{12,8},{13,9},{14,10},{15,11},{20,16},{21,... | collective-permute-start | bytes 86024 | tf_op jit(solution)/shard_map/ppermute | solution.py:743
  305.7 248.2 %reduce-scatter.5.cloned.1.call-start = ((), (), s32[]{:S(2)}) async-start(), calls=%async_computation.4 | async-start | bytes 2359296 | tf_op jit(solution)/shard_map/reduce_scatter | solution.py:1016
  306.9 28.9 %collective-permute-start.39 = (bf16[512,1024]{1,0:T(8,128)(2,1)S(1)}, bf16[512,1024]{1,0:T(8,128)(2,1)}, u32[]{:S(2)}, u32[]{:S(2)}) collective-permute-start(bf16[512,1024]{1,0:T(8,128)(2,1)S(1)} %copy-done.9), channel_id=1, source_target_pairs={{0,1},{3,2},{4,5},{7,6},{8,9},{11,10},{12,13},{15,14},{16,17},{19,... | collective-permute-start | bytes 3145736 | tf_op jit(solution)/shard_map/ppermute | solution.py:792
  314.1 51.1 %collective-permute-start.29 = (bf16[512,1024]{1,0:T(8,128)(2,1)S(1)}, bf16[512,1024]{1,0:T(8,128)(2,1)}, u32[]{:S(2)}, u32[]{:S(2)}) collective-permute-start(bf16[512,1024]{1,0:T(8,128)(2,1)S(1)} %copy-done.3), channel_id=1, source_target_pairs={{1,0},{2,3},{5,4},{6,7},{9,8},{10,11},{13,12},{14,15},{17,16},{18,... | collective-permute-start | bytes 3145736 | tf_op jit(solution)/shard_map/ppermute | solution.py:802
  315.4 42.9 %collective-permute-start.36 = (bf16[512,1024]{1,0:T(8,128)(2,1)}, bf16[512,1024]{1,0:T(8,128)(2,1)}, u32[]{:S(2)}, u32[]{:S(2)}) collective-permute-start(bf16[512,1024]{1,0:T(8,128)(2,1)} %get-tuple-element.149.refs_0_), channel_id=1, source_target_pairs={{0,1},{3,2},{4,5},{7,6},{8,9},{11,10},{12,13},{15,14},{16,17},{19,... | collective-permute-start | bytes 3145736 | tf_op jit(solution)/shard_map/ppermute | solution.py:792
  322.8 18.4 %collective-permute-start.42 = (f32[5120]{0:T(1024)S(1)}, f32[5120]{0:T(1024)S(1)}, u32[]{:S(2)}, u32[]{:S(2)}) collective-permute-start(f32[5120]{0:T(1024)S(1)} %pad_maximum_fusion.5), channel_id=1, source_target_pairs={{0,4},{4,0},{1,5},{5,1},{2,6},{6,2},{3,7},{7,3},{8,12},{12,8},{9,1... | collective-permute-start | bytes 61448 | tf_op jit(solution)/shard_map/ppermute | solution.py:758
  323.2 48.2 %collective-permute-start.23 = (bf16[512,1024]{1,0:T(8,128)(2,1)S(1)}, bf16[512,1024]{1,0:T(8,128)(2,1)}, u32[]{:S(2)}, u32[]{:S(2)}) collective-permute-start(bf16[512,1024]{1,0:T(8,128)(2,1)S(1)} %copy-done.1), channel_id=1, source_target_pairs={{1,2},{2,1},{5,6},{6,5},{9,10},{10,9},{13,14},{14,13},{17,18},{18,... | collective-permute-start | bytes 3145736 | tf_op jit(solution)/shard_map/ppermute | solution.py:797
  335.8 45.0 %collective-permute-start.30 = (bf16[512,1024]{1,0:T(8,128)(2,1)}, bf16[512,1024]{1,0:T(8,128)(2,1)}, u32[]{:S(2)}, u32[]{:S(2)}) collective-permute-start(bf16[512,1024]{1,0:T(8,128)(2,1)} %get-tuple-element.145.refs_0_), channel_id=1, source_target_pairs={{0,1},{3,2},{4,5},{7,6},{8,9},{11,10},{12,13},{15,14},{16,17},{19,... | collective-permute-start | bytes 3145736 | tf_op jit(solution)/shard_map/ppermute | solution.py:792
  341.2 62.0 %collective-permute-start.33 = (bf16[512,1024]{1,0:T(8,128)(2,1)}, bf16[512,1024]{1,0:T(8,128)(2,1)}, u32[]{:S(2)}, u32[]{:S(2)}) collective-permute-start(bf16[512,1024]{1,0:T(8,128)(2,1)} %get-tuple-element.148.refs_0_), channel_id=1, source_target_pairs={{0,1},{3,2},{4,5},{7,6},{8,9},{11,10},{12,13},{15,14},{16,17},{19,... | collective-permute-start | bytes 3145736 | tf_op jit(solution)/shard_map/ppermute | solution.py:792
  358.3 5.2 collective-permute-start.43
  363.6 46.3 %collective-permute-start.37 = (bf16[512,1024]{1,0:T(8,128)(2,1)}, bf16[512,1024]{1,0:T(8,128)(2,1)}, u32[]{:S(2)}, u32[]{:S(2)}) collective-permute-start(bf16[512,1024]{1,0:T(8,128)(2,1)} %join.28.refs_0_), channel_id=1, source_target_pairs={{1,2},{2,1},{5,6},{6,5},{9,10},{10,9},{13,14},{14,13},{17,18},{18,... | collective-permute-start | bytes 3145736 | tf_op jit(solution)/shard_map/ppermute | solution.py:797
  365.2 10.0 %collective-permute-start.44 = (f32[5120]{0:T(1024)S(1)}, f32[5120]{0:T(1024)S(1)}, u32[]{:S(2)}, u32[]{:S(2)}) collective-permute-start(f32[5120]{0:T(1024)S(1)} %add.161), channel_id=1, source_target_pairs={{0,16},{8,24},{16,0},{24,8},{1,17},{9,25},{17,1},{25,9},{2,18},{10... | collective-permute-start | bytes 61448 | tf_op jit(solution)/shard_map/ppermute | solution.py:758
  371.4 60.7 %collective-permute-start.28 = (bf16[512,1024]{1,0:T(8,128)(2,1)S(1)}, bf16[512,1024]{1,0:T(8,128)(2,1)}, u32[]{:S(2)}, u32[]{:S(2)}) collective-permute-start(bf16[512,1024]{1,0:T(8,128)(2,1)S(1)} %copy-done.2), channel_id=1, source_target_pairs={{1,0},{2,3},{5,4},{6,7},{9,8},{10,11},{13,12},{14,15},{17,16},{18,... | collective-permute-start | bytes 3145736 | tf_op jit(solution)/shard_map/ppermute | solution.py:802
  375.1 45.6 %collective-permute-start.40 = (bf16[512,1024]{1,0:T(8,128)(2,1)}, bf16[512,1024]{1,0:T(8,128)(2,1)S(1)}, u32[]{:S(2)}, u32[]{:S(2)}) collective-permute-start(bf16[512,1024]{1,0:T(8,128)(2,1)} %join.30.refs_0_), channel_id=1, source_target_pairs={{1,2},{2,1},{5,6},{6,5},{9,10},{10,9},{13,14},{14,13},{17,18},{18,... | collective-permute-start | bytes 3145736 | tf_op jit(solution)/shard_map/ppermute | solution.py:797
  383.3 41.2 %collective-permute-start.31 = (bf16[512,1024]{1,0:T(8,128)(2,1)}, bf16[512,1024]{1,0:T(8,128)(2,1)}, u32[]{:S(2)}, u32[]{:S(2)}) collective-permute-start(bf16[512,1024]{1,0:T(8,128)(2,1)} %join.24.refs_0_), channel_id=1, source_target_pairs={{1,2},{2,1},{5,6},{6,5},{9,10},{10,9},{13,14},{14,13},{17,18},{18,... | collective-permute-start | bytes 3145736 | tf_op jit(solution)/shard_map/ppermute | solution.py:797
  405.7 22.6 %collective-permute-start.34 = (bf16[512,1024]{1,0:T(8,128)(2,1)}, bf16[512,1024]{1,0:T(8,128)(2,1)}, u32[]{:S(2)}, u32[]{:S(2)}) collective-permute-start(bf16[512,1024]{1,0:T(8,128)(2,1)} %join.26.refs_0_), channel_id=1, source_target_pairs={{1,2},{2,1},{5,6},{6,5},{9,10},{10,9},{13,14},{14,13},{17,18},{18,... | collective-permute-start | bytes 3145736 | tf_op jit(solution)/shard_map/ppermute | solution.py:797
  409.9 23.5 %collective-permute-start.45 = (f32[34176]{0:T(1024)S(1)}, f32[34176]{0:T(1024)S(1)}, u32[]{:S(2)}, u32[]{:S(2)}) collective-permute-start(f32[34176]{0:T(1024)S(1)} %pad_maximum_fusion), channel_id=1, source_target_pairs={{0,1},{1,0},{2,3},{3,2},{4,5},{5,4},{6,7},{7,6},{8,9},{9,8},{10,11... | collective-permute-start | bytes 410120 | tf_op jit(solution)/shard_map/ppermute | solution.py:758
  420.8 28.0 %collective-permute-start.27 = (bf16[512,1024]{1,0:T(8,128)(2,1)S(1)}, bf16[512,1024]{1,0:T(8,128)(2,1)S(1)}, u32[]{:S(2)}, u32[]{:S(2)}) collective-permute-start(bf16[512,1024]{1,0:T(8,128)(2,1)S(1)} %copy-done.7), channel_id=1, source_target_pairs={{1,0},{2,3},{5,4},{6,7},{9,8},{10,11},{13,12},{14,15},{17,16},{18,... | collective-permute-start | bytes 3145736 | tf_op jit(solution)/shard_map/ppermute | solution.py:802
  424.6 76.8 %collective-permute-start.38 = (bf16[512,1024]{1,0:T(8,128)(2,1)}, bf16[512,1024]{1,0:T(8,128)(2,1)S(1)}, u32[]{:S(2)}, u32[]{:S(2)}) collective-permute-start(bf16[512,1024]{1,0:T(8,128)(2,1)} %join.29.refs_4_), channel_id=1, source_target_pairs={{1,0},{2,3},{5,4},{6,7},{9,8},{10,11},{13,12},{14,15},{17,16},{18,... | collective-permute-start | bytes 3145736 | tf_op jit(solution)/shard_map/ppermute | solution.py:802
  428.3 68.4 %collective-permute-start.41 = (bf16[512,1024]{1,0:T(8,128)(2,1)}, bf16[512,1024]{1,0:T(8,128)(2,1)S(1)}, u32[]{:S(2)}, u32[]{:S(2)}) collective-permute-start(bf16[512,1024]{1,0:T(8,128)(2,1)} %join.31.refs_4_), channel_id=1, source_target_pairs={{1,0},{2,3},{5,4},{6,7},{9,8},{10,11},{13,12},{14,15},{17,16},{18,... | collective-permute-start | bytes 3145736 | tf_op jit(solution)/shard_map/ppermute | solution.py:802
  432.1 112.8 %collective-permute-start.32 = (bf16[512,1024]{1,0:T(8,128)(2,1)}, bf16[512,1024]{1,0:T(8,128)(2,1)S(1)}, u32[]{:S(2)}, u32[]{:S(2)}) collective-permute-start(bf16[512,1024]{1,0:T(8,128)(2,1)} %join.25.refs_4_), channel_id=1, source_target_pairs={{1,0},{2,3},{5,4},{6,7},{9,8},{10,11},{13,12},{14,15},{17,16},{18,... | collective-permute-start | bytes 3145736 | tf_op jit(solution)/shard_map/ppermute | solution.py:802
  433.4 106.9 %collective-permute-start.35 = (bf16[512,1024]{1,0:T(8,128)(2,1)}, bf16[512,1024]{1,0:T(8,128)(2,1)S(1)}, u32[]{:S(2)}, u32[]{:S(2)}) collective-permute-start(bf16[512,1024]{1,0:T(8,128)(2,1)} %join.27.refs_4_), channel_id=1, source_target_pairs={{1,0},{2,3},{5,4},{6,7},{9,8},{10,11},{13,12},{14,15},{17,16},{18,... | collective-permute-start | bytes 3145736 | tf_op jit(solution)/shard_map/ppermute | solution.py:802
  448.8 102.7 %collective-permute-start.46 = (f32[34176]{0:T(1024)S(1)}, f32[34176]{0:T(1024)S(1)}, u32[]{:S(2)}, u32[]{:S(2)}) collective-permute-start(f32[34176]{0:T(1024)S(1)} %fusion.23), channel_id=1, source_target_pairs={{0,2},{1,3},{2,0},{3,1},{4,6},{5,7},{6,4},{7,5},{8,10},{9,11},{10,... | collective-permute-start | bytes 410120 | tf_op jit(solution)/shard_map/ppermute | solution.py:758
  (52 other events, 618.7 us)
Sparse Core Ops, SparseCore 0:
  21.8 22.8 all-gather.1
  305.8 61.5 reduce-scatter.2
  371.6 41.2 reduce-scatter.4
